TPU v7x, 256 devices: a whole 4x4x8 slice. The times are simulated.
256 devices in a mesh: mem: 16 (over y_hi, x, core), sp: 16 (over z, y_lo).
Axes of the slice: x: 4, y: 4 (y_hi: 2, y_lo: 2; y = y_hi * 2 + y_lo), z: 8, core: 2. Of those that a mesh axis runs over, the one named last changes fastest.
Arguments:
- background_samples: bfloat16 [1024, 65536], P('mem', 'sp'), may hold values from -8 to 8
- sensor_cell_offsets: int32 [131072], P('sp'), may hold values from 0 to 4095
- sensor_data: float32 [131072], P('sp'), may hold values from -6 to 6
- sensor_sigma_list: float32 [131072], P('sp'), may hold values from 1.5 to 2.5
Outputs:
- analysis: bfloat16 [1024, 65536], P('mem', 'sp')
Inputs may be any that keep to these rules, and one draw needn't show every extreme that they name: Observation j reads state row (j // 8192) * 4096 + sensor_cell_offsets[j].
All inputs are finite; a program needn't handle non-finite values.
Results may differ from a plain program's by a relative error of at most 0.0064.
Values may be sent and summed in bfloat16 or wider, within the bound.
No kernel may reach another device: no remote copies, remote signals or barrier semaphores. Data moves between devices by JAX's collectives and lax.ppermute only.
A program may use at most 128 MiB of HBM per device.

v0:
```python
import math

import jax
import jax.numpy as jnp
from jax import lax
from jax.sharding import PartitionSpec as P


def own_columns(factor, mean_weights, member_index, realization_vectors, sample_cloud, root_scale):
    picker = (
        jnp.arange(sample_cloud, dtype=jnp.int32)[:, None]
        == member_index * realization_vectors
        + jnp.arange(realization_vectors, dtype=jnp.int32)[None, :]
    ).astype(jnp.float32)
    root_cols = jax.scipy.linalg.solve_triangular(factor, picker, trans=1, lower=True)
    return (root_cols * root_scale + mean_weights[:, None]).astype(jnp.bfloat16)


def per_device(background_samples, sensor_cell_offsets, sensor_data, sensor_sigma_list):
    realization_vectors = background_samples.shape[0]
    groups = lax.axis_size("mem")
    sample_cloud = realization_vectors * groups
    member_index = lax.axis_index("mem")
    running_block_tally = jnp.sum(background_samples, axis=0, dtype=jnp.float32)
    predicted_centroid = lax.psum(running_block_tally, "mem") / sample_cloud
    centred_spread_matrix = (
        background_samples.astype(jnp.float32) - predicted_centroid[None, :]
    ).astype(jnp.bfloat16)
    picked = jnp.take(centred_spread_matrix, sensor_cell_offsets, axis=1)
    scaled = (picked.astype(jnp.float32) / sensor_sigma_list[None, :]).astype(jnp.bfloat16)
    misfit_residual = (
        sensor_data - jnp.take(predicted_centroid, sensor_cell_offsets)
    ) / sensor_sigma_list
    gram_cols = jnp.einsum(
        "ko,lo->kl",
        lax.all_gather(scaled, "mem", axis=0, tiled=True),
        scaled,
        preferred_element_type=jnp.float32,
    )
    drive_cols = jnp.dot(
        scaled.astype(jnp.float32), misfit_residual, precision=lax.Precision.HIGHEST
    )
    gram_cols, drive_cols = lax.psum((gram_cols, drive_cols), "sp")
    gram_matrix, obs_drive = (
        lax.all_gather(gram_cols, "mem", axis=1, tiled=True),
        lax.all_gather(drive_cols, "mem", axis=0, tiled=True),
    )
    gram_matrix = gram_matrix + (sample_cloud - 1) * jnp.eye(sample_cloud, dtype=jnp.float32)
    factor = jnp.linalg.cholesky(gram_matrix)
    mean_weights = jax.scipy.linalg.cho_solve((factor, True), obs_drive)
    root_scale = math.sqrt(sample_cloud - 1)
    transform_cols = own_columns(
        factor, mean_weights, member_index, realization_vectors, sample_cloud, root_scale
    )
    update_shift = jnp.einsum(
        "kl,kr->lr",
        transform_cols,
        lax.all_gather(centred_spread_matrix, "mem", axis=0, tiled=True),
        preferred_element_type=jnp.float32,
    )
    return (predicted_centroid[None, :] + update_shift).astype(jnp.bfloat16)


def solution(mesh):
    return jax.shard_map(
        per_device,
        mesh=mesh,
        in_specs=(P("mem", "sp"), P("sp"), P("sp"), P("sp")),
        out_specs=P("mem", "sp"),
        check_vma=False,
    )
```

profile of v0, /device:TPU:1, one launch (start us, length us, event | category | flops | bytes accessed | tf_op | source)
XLA Modules:
  0.0 864.9 jit_solution(13982839373793738847)
XLA Ops:
  7.7 65.2 %psum.21 = f32[4096]{0:T(1024)S(1)} all-reduce(f32[4096]{0:T(1024)S(1)} %convert_reduce_fusion), channel_id=1, replica_groups=mesh['mem'=16,'sp'=16] {'mem'}, use_global_device_ids=true, to_apply=%region_1.0 | all-reduce | flops 4096 | bytes 32768 | tf_op jit(solution)/shard_map/psum | solution.py:25
  75.3 45.5 %gather_fusion.1 = f32[8192]{0:T(1024)S(1)} fusion(f32[4096]{0:T(1024)S(1)} %broadcast_multiply_fusion, s32[8192]{0:T(1024)S(1)} %fusion.112), kind=kCustom, calls=%fused_computation.1 | custom fusion | bytes 98304 | tf_op jit(solution)/shard_map/jit(_take)/gather | solution.py:32
  120.9 29.2 %gather_fusion = bf16[8192,64]{1,0:T(8,128)(2,1)} fusion(bf16[64,4096]{0,1:T(8,128)(2,1)S(1)} %copy.41, s32[8192]{0:T(1024)S(1)} %fusion.112), kind=kCustom, calls=%fused_computation | custom fusion | bytes 2129920 | tf_op jit(solution)/shard_map/jit(_take)/gather | solution.py:29
  150.1 5.6 fusion.198
  157.4 119.6 %all-gather.4.cloned.1.call-done = bf16[1024,8192]{1,0:T(8,128)(2,1)} async-done(((bf16[64,8192]{1,0:T(8,128)(2,1)}), bf16[1024,8192]{1,0:T(8,128)(2,1)}) %all-gather.4.cloned.1.call-update) | async-done | bytes 16777232 | tf_op jit(solution)/shard_map/all_gather | solution.py:36
  277.0 10.0 %fusion.159 = f32[1024,64]{0,1:T(8,128)} fusion(bf16[1024,8192]{1,0:T(8,128)(2,1)} %all-gather.4.cloned.1.call-done, f32[8192]{0:T(1024)S(1)} %copy-done.4, bf16[8192,64]{1,0:T(8,128)(2,1)} %gather_fusion, pred[8192]{0:T(1024)(128)(4,1)S(1)} %get-tuple-element.34), kind=kOutput, calls=%fused_computation.334 | convolution fusion | flops 1075838976 | bytes 18128896 | tf_op jit(solution)/shard_map/ko,lo->kl/dot_general | solution.py:34
  287.1 123.2 %all-reduce.4.cloned.1.call-done = f32[1024,64]{0,1:T(8,128)} async-done(((f32[1024,64]{0,1:T(8,128)}), f32[1024,64]{0,1:T(8,128)}) %all-reduce.4.cloned.1.call-update) | async-done | bytes 262160 | tf_op jit(solution)/shard_map/psum | solution.py:43
  413.8 26.5 %psum.23 = f32[64]{0:T(128)S(1)} all-reduce(f32[64]{0:T(128)S(1)} %convolution_bitcast_fusion.23), channel_id=1, replica_groups=mesh['mem'=16,'sp'=16] {'sp'}, use_global_device_ids=true, to_apply=%region_19.20 | all-reduce | flops 64 | bytes 512 | tf_op jit(solution)/shard_map/psum | solution.py:43
  441.9 51.0 %all-reduce.1 = f32[1024]{0:T(1024)S(1)} all-reduce(f32[1024]{0:T(1024)S(1)} %dynamic-update-slice.47), channel_id=1, replica_groups=mesh['mem'=16,'sp'=16] {'mem'}, use_global_device_ids=true, to_apply=%add.1 | all-reduce | flops 1024 | bytes 8192
  493.0 4.8 select_add_fusion
  497.8 6.0 copy.43
  503.7 4.5 fusion.1
  510.2 11.7 %cholesky.222 = f32[128,128]{1,0:T(8,128)S(1)} custom-call(f32[128,128]{1,0:T(8,128)S(1)} %cholesky.577), custom_call_target="Cholesky" | custom-call | tf_op jit(solution)/shard_map/jit(cholesky)/cholesky | solution.py:49
  522.0 9.8 %custom-call.69 = f32[1,128,128]{1,2,0:T(8,128)S(1)} custom-call(f32[1,128,128]{2,1,0:T(8,128)S(1)} %get-tuple-element.50), custom_call_target="InvertDiagBlocksLowerTriangular" | custom-call | tf_op jit(solution)/shard_map/jit(cholesky)/cholesky | solution.py:49
  534.9 11.7 %cholesky.243 = f32[128,128]{1,0:T(8,128)S(1)} custom-call(f32[128,128]{1,0:T(8,128)S(1)} %cholesky.581), custom_call_target="Cholesky" | custom-call | tf_op jit(solution)/shard_map/jit(cholesky)/cholesky | solution.py:49
  549.7 9.8 %custom-call.70 = f32[1,128,128]{1,2,0:T(8,128)S(1)} custom-call(f32[1,128,128]{2,1,0:T(8,128)S(1)} %get-tuple-element.48), custom_call_target="InvertDiagBlocksLowerTriangular" | custom-call | tf_op jit(solution)/shard_map/jit(cholesky)/cholesky | solution.py:49
  565.1 11.7 %cholesky.466 = f32[128,128]{1,0:T(8,128)S(1)} custom-call(f32[128,128]{1,0:T(8,128)S(1)} %cholesky.586), custom_call_target="Cholesky" | custom-call | tf_op jit(solution)/shard_map/jit(cholesky)/cholesky | solution.py:49
  577.6 9.8 %custom-call.71 = f32[1,128,128]{1,2,0:T(8,128)S(1)} custom-call(f32[1,128,128]{2,1,0:T(8,128)S(1)} %get-tuple-element.46), custom_call_target="InvertDiagBlocksLowerTriangular" | custom-call | tf_op jit(solution)/shard_map/jit(cholesky)/cholesky | solution.py:49
  588.6 3.3 convolution_subtract_fusion.2
  592.0 11.7 %cholesky.485 = f32[128,128]{1,0:T(8,128)S(1)} custom-call(f32[128,128]{1,0:T(8,128)S(1)} %cholesky.591), custom_call_target="Cholesky" | custom-call | tf_op jit(solution)/shard_map/jit(cholesky)/cholesky | solution.py:49
  604.5 9.8 %custom-call.72 = f32[1,128,128]{1,2,0:T(8,128)S(1)} custom-call(f32[1,128,128]{2,1,0:T(8,128)S(1)} %get-tuple-element.44), custom_call_target="InvertDiagBlocksLowerTriangular" | custom-call | tf_op jit(solution)/shard_map/jit(cholesky)/cholesky | solution.py:49
  618.6 12.1 %cholesky.504 = f32[128,128]{1,0:T(8,128)S(1)} custom-call(f32[128,128]{1,0:T(8,128)S(1)} %cholesky.596), custom_call_target="Cholesky" | custom-call | tf_op jit(solution)/shard_map/jit(cholesky)/cholesky | solution.py:49
  631.4 9.8 %custom-call.73 = f32[1,128,128]{1,2,0:T(8,128)S(1)} custom-call(f32[1,128,128]{2,1,0:T(8,128)S(1)} %get-tuple-element.42), custom_call_target="InvertDiagBlocksLowerTriangular" | custom-call | tf_op jit(solution)/shard_map/jit(cholesky)/cholesky | solution.py:49
  645.5 11.7 %cholesky.524 = f32[128,128]{1,0:T(8,128)S(1)} custom-call(f32[128,128]{1,0:T(8,128)S(1)} %cholesky.601), custom_call_target="Cholesky" | custom-call | tf_op jit(solution)/shard_map/jit(cholesky)/cholesky | solution.py:49
  658.0 9.8 %custom-call.74 = f32[1,128,128]{1,2,0:T(8,128)S(1)} custom-call(f32[1,128,128]{2,1,0:T(8,128)S(1)} %get-tuple-element.40), custom_call_target="InvertDiagBlocksLowerTriangular" | custom-call | tf_op jit(solution)/shard_map/jit(cholesky)/cholesky | solution.py:49
  671.6 11.7 %cholesky.544 = f32[128,128]{1,0:T(8,128)S(1)} custom-call(f32[128,128]{1,0:T(8,128)S(1)} %cholesky.606), custom_call_target="Cholesky" | custom-call | tf_op jit(solution)/shard_map/jit(cholesky)/cholesky | solution.py:49
  684.1 9.8 %custom-call.75 = f32[1,128,128]{1,2,0:T(8,128)S(1)} custom-call(f32[1,128,128]{2,1,0:T(8,128)S(1)} %get-tuple-element.38), custom_call_target="InvertDiagBlocksLowerTriangular" | custom-call | tf_op jit(solution)/shard_map/jit(cholesky)/cholesky | solution.py:49
  696.9 11.7 %cholesky.562 = f32[128,128]{1,0:T(8,128)S(1)} custom-call(f32[128,128]{1,0:T(8,128)S(1)} %convolution_subtract_fusion.6), custom_call_target="Cholesky" | custom-call | tf_op jit(solution)/shard_map/jit(cholesky)/cholesky | solution.py:49
  718.8 4.9 select_select_fusion
  723.7 24.5 %while.1 = (s32[]{:T(128)}, f32[1024,1024]{0,1:T(8,128)}, s32[8,2]{0,1:T(2,128)S(1)}, f32[8,128,128]{2,1,0:T(8,128)S(1)}, s32[]{:T(128)}) while((s32[]{:T(128)}, f32[1024,1024]{0,1:T(8,128)}, s32[8,2]{0,1:T(2,128)S(1)}, f32[8,128,128]{2,1,0:T(8,128)S(1)}, s32[]{:T(128)}) %tuple.56), condition=%wide.while_cond, body=%wide.while_body.sunk | while | flops 2 | bytes 393321 | solution.py:15
  748.2 78.8 %custom-call.76 = f32[8,128,128]{1,2,0:T(8,128)S(1)} custom-call(f32[8,128,128]{2,1,0:T(8,128)S(1)} %get-tuple-element.12), custom_call_target="InvertDiagBlocksLowerTriangular" | custom-call | tf_op jit(solution)/shard_map/jit(_solve_triangular)/triangular_solve | solution.py:15
  852.4 5.7 fusion
  (224 shorter events, 98.3 us)
Async XLA Ops:
  6.5 270.5 %all-gather.4.cloned.1.call-start = ((), (), s32[]{:S(2)}) async-start(), calls=%async_computation | async-start | bytes 17825792 | tf_op jit(solution)/shard_map/all_gather | solution.py:36
  74.0 46.8 %copy-start.3 = (bf16[64,4096]{1,0:T(8,128)(2,1)}, bf16[64,4096]{1,0:T(8,128)(2,1)S(1)}, u32[]{:S(2)}) copy-start(bf16[64,4096]{1,0:T(8,128)(2,1)S(1)} %fusion.31) | copy-start | bytes 1572868
  120.8 29.3 %copy-start.4 = (f32[8192]{0:T(1024)S(1)}, f32[8192]{0:T(1024)}, u32[]{:S(2)}) copy-start(f32[8192]{0:T(1024)} %param.7) | copy-start | bytes 98308
  120.8 29.2 %copy-start.5 = (s32[8192]{0:T(1024)S(1)}, s32[8192]{0:T(1024)}, u32[]{:S(2)}) copy-start(s32[8192]{0:T(1024)} %param.5) | copy-start | bytes 98308
  120.8 29.2 %copy-start.6 = (f32[8192]{0:T(1024)S(1)}, f32[8192]{0:T(1024)}, u32[]{:S(2)}) copy-start(f32[8192]{0:T(1024)} %param.6) | copy-start | bytes 98308
  157.4 253.5 %copy-start.2 = (bf16[8192,64]{1,0:T(8,128)(2,1)S(1)}, bf16[8192,64]{1,0:T(8,128)(2,1)}, u32[]{:S(2)}) copy-start(bf16[8192,64]{1,0:T(8,128)(2,1)} %gather_fusion) | copy-start | bytes 3145732
  157.4 252.9 %all-reduce.4.cloned.1.call-start = ((), (), s32[]{:S(2)}) async-start(), calls=%async_computation.1 | async-start | bytes 524288 | tf_op jit(solution)/shard_map/psum | solution.py:43
  287.0 205.9 %all-gather.6.cloned.1.call-start = ((), (), s32[]{:S(2)}) async-start(), calls=%async_computation.2 | async-start | bytes 4456448 | tf_op jit(solution)/shard_map/all_gather | solution.py:45
  410.3 442.1 %all-gather.8.cloned.1.call-start = ((), (), s32[]{:S(2)}) async-start(), calls=%async_computation.3 | async-start | bytes 8912896 | tf_op jit(solution)/shard_map/all_gather | solution.py:58
  410.9 29.4 %copy-start.7 = (u32[256]{0:T(256)S(1)}, u32[256]{0:T(256)}, u32[]{:S(2)}) copy-start(u32[256]{0:T(256)} %constant.357) | copy-start | bytes 3076
  508.2 2.0 copy-start.1
  827.0 19.3 %copy-start = (f32[1024,1024]{0,1:T(8,128)S(1)}, f32[1024,1024]{0,1:T(8,128)}, u32[]{:S(2)}) copy-start(f32[1024,1024]{0,1:T(8,128)} %get-tuple-element.141) | copy-start | bytes 12582916
Sparse Core Ops, SparseCore 0:
  157.5 119.4 all-gather.3
  287.2 123.0 all-reduce.3
  413.4 71.6 all-gather.5
  488.0 76.9 all-gather.7
where the time goes:
time: 872 us; the launch traced here: 865 us
  other arithmetic  269 us (31%)
  waiting for transfers between devices  243 us (28%)
  blocking collectives  143 us (16%)
  local copies, waits for them, and re-layouts  119 us (14%)
  matrix products  70.2 us (8%)
  between operations  19.9 us (2%)
    another operation x30, other arithmetic, per_device(): factor = jnp.linalg.cholesky(gram_matrix)  168 us
    psum x1, waiting for transfers between devices, per_device(): gram_cols, drive_cols = lax.psum((gram_cols, drive_cols), 'sp')  123 us
    all_gather x1, waiting for transfers between devices, per_device(): lax.all_gather(scaled, 'mem', axis=0, tiled=True)  120 us
    another operation x3, other arithmetic, own_columns(): jax.scipy.linalg.solve_triangular(factor, picker, trans=1, lower=True)  83.7 us
    psum x1, blocking collectives, per_device(): predicted_centroid = lax.psum(running_block_tally, 'mem') / sample_cloud  65.2 us
    unnamed x1, blocking collectives  51 us
    gather x1, local copies, waits for them, and re-layouts, per_device(): jnp.take(predicted_centroid, sensor_cell_offsets)  45.5 us
    gather x1, local copies, waits for them, and re-layouts, per_device(): picked = jnp.take(centred_spread_matrix, sensor_cell_offsets, axis=1)  29.2 us
  transfers between devices with their start and end apart: 4, of which 2 were waited for; matrix products, arithmetic and copies ran while one was open for 41% of the time, Pallas kernels for 0%

commit v1 on v0

v1 whole, which is shorter than its diff:
```python
import math

import jax
import jax.numpy as jnp
from jax import lax
from jax.experimental import pallas as pl
from jax.experimental.pallas import tpu as pltpu
from jax.sharding import Mesh, PartitionSpec as P

F32 = jnp.float32
BF = jnp.bfloat16
N = 1024
CELLS = 4096
OBS = 8192
HALF = CELLS // 2
NB = 128
SB = 8
NK = N // NB
NT = 5
ROWS = 384
DRIVE = NT * 64
VMEM = pl.BlockSpec(memory_space=pltpu.VMEM)
SMEM = pl.BlockSpec(memory_space=pltpu.SMEM)
NTDOT = (((1,), (1,)), ((), ()))
TNDOT = (((0,), (0,)), ((), ()))


def params(mib):
    return pltpu.CompilerParams(vmem_limit_bytes=mib * 2**20)


def split3(x):
    h = x.astype(BF)
    r = x - h.astype(F32)
    m = r.astype(BF)
    return h, m, (r - m.astype(F32)).astype(BF)


def at(i, size):
    return pl.ds(pl.multiple_of(i * size, size), size)


def obs_kernel(scal, off_ref, data_ref, sigma_ref, out_ref, lhs, oh):
    core = scal[2]
    hi_iota = lax.broadcasted_iota(jnp.int32, (16, NB), 0) + core * 16
    lo_iota = lax.broadcasted_iota(jnp.int32, (NB, NB), 0)
    for r in range(OBS // NB):
        off = off_ref[r : r + 1, :]
        sigma = sigma_ref[r : r + 1, :]
        w = 1.0 / (sigma * sigma)
        s = data_ref[r : r + 1, :] * w
        mask = lax.shift_right_logical(off, 7) == hi_iota
        cols = slice(r * NB, (r + 1) * NB)
        for i, v in enumerate(split3(w) + split3(s)):
            v = jnp.broadcast_to(v.astype(F32), (16, NB))
            lhs[16 * i : 16 * i + 16, cols] = jnp.where(mask, v, 0.0).astype(BF)
        oh[:, cols] = jnp.where((off & 127) == lo_iota, 1.0, 0.0).astype(BF)
    t = lax.dot_general(lhs[...], oh[...], NTDOT, preferred_element_type=F32)
    w = t[0:16] + t[16:32] + t[32:48]
    s = t[48:64] + t[64:80] + t[80:96]
    out_ref[...] = jnp.zeros_like(out_ref)
    for h in range(16):
        out_ref[0:1, h * NB : (h + 1) * NB] = w[h : h + 1]
        out_ref[1:2, h * NB : (h + 1) * NB] = s[h : h + 1]


def obs_sums(scal, off, data, sigma):
    shape = (OBS // NB, NB)
    return pl.pallas_call(
        obs_kernel,
        out_shape=jax.ShapeDtypeStruct((8, HALF), F32),
        in_specs=[SMEM, VMEM, VMEM, VMEM],
        out_specs=VMEM,
        scratch_shapes=[pltpu.VMEM((96, OBS), BF), pltpu.VMEM((NB, OBS), BF)],
        compiler_params=params(24),
        cost_estimate=pl.CostEstimate(flops=2 * 96 * NB * OBS, bytes_accessed=200000, transcendentals=0),
        name="obs_sums",
    )(scal, off.reshape(shape), data.reshape(shape), sigma.reshape(shape))


SHIFTS = [(sx, sy) for sy in range(2) for sx in range(4)]


def chip_of(scal, sx, sy):
    return ((scal[0] - sy + 2) % 2) * 4 + (scal[1] - sx + 4) % 4


def gram_kernel(scal, ws_ref, *refs):
    pieces = refs[:8]
    keep, send, mean_ref, b = refs[8:]
    core = scal[2]
    me = scal[0] * 4 + scal[1]
    width = 256

    def cols_body(c, carry):
        cols = at(c, width)
        total = jnp.zeros((1, width), F32)
        for p in pieces:
            total = total + jnp.sum(p[:, cols].astype(F32), axis=0, keepdims=True)
        mean = total * (1.0 / N)
        mean_ref[:, cols] = jnp.broadcast_to(mean, (8, width))
        root = jnp.sqrt(ws_ref[0:1, cols])
        for p, (sx, sy) in zip(pieces, SHIFTS):
            b[at(chip_of(scal, sx, sy), NB), cols] = ((p[:, cols].astype(F32) - mean) * root).astype(BF)
        return carry

    lax.fori_loop(0, HALF // width, cols_body, 0)
    w = ws_ref[0:1, :]
    d = jnp.where(w > 0.0, (ws_ref[1:2, :] - mean_ref[0:1, :] * w) * lax.rsqrt(jnp.where(w > 0.0, w, 1.0)), 0.0)
    d = jnp.concatenate([x.astype(F32) for x in split3(d)] + [jnp.zeros((13, HALF), F32)], axis=0).astype(BF)
    mine = b[at(2 * me + core, 64), :]
    other = b[at(2 * me + 1 - core, 64), :]
    lhs = jnp.concatenate([mine, other], axis=0)
    for i in range(NT):
        rhs = b[at((me + i) % NK, NB), :]
        g = lax.dot_general(lhs, rhs, NTDOT, preferred_element_type=F32)
        keep[64 * i : 64 * i + 64, :] = g[:64]
        send[64 * i : 64 * i + 64, :] = g[64:]
        if i == 0:
            drive = lax.dot_general(d, rhs, NTDOT, preferred_element_type=F32)
            drive = jnp.broadcast_to(jnp.sum(drive, axis=0, keepdims=True), (8, NB))
            for out in (keep, send):
                out[DRIVE : DRIVE + 8, :] = drive
                out[DRIVE + 8 :, :] = jnp.zeros((ROWS - DRIVE - 8, NB), F32)


def gram_part(scal, ws, pieces):
    part = jax.ShapeDtypeStruct((ROWS, NB), F32)
    return pl.pallas_call(
        gram_kernel,
        out_shape=(part, part, jax.ShapeDtypeStruct((8, HALF), F32)),
        in_specs=[SMEM] + [VMEM] * 9,
        out_specs=(VMEM, VMEM, VMEM),
        scratch_shapes=[pltpu.VMEM((N, HALF), BF)],
        compiler_params=params(32),
        cost_estimate=pl.CostEstimate(flops=2 * NB * NB * NT * HALF, bytes_accessed=5 * 2**20, transcendentals=0),
        name="gram_part",
    )(scal, ws, *pieces)


def diag_inverse(dz, vout):
    for j in range(NB // SB):
        r0 = j * SB
        rs = [jnp.broadcast_to(dz[r0 + p : r0 + p + 1, 0:NB], (SB, NB)) for p in range(SB)]
        rw = [jnp.broadcast_to(dz[r0 + p : r0 + p + 1, NB : 2 * NB], (SB, NB)) for p in range(SB)]
        e = [[jnp.broadcast_to(rs[q][:, r0 + p : r0 + p + 1], (SB, NB)) for p in range(q + 1)] for q in range(SB)]
        groups = range(j + 1, NB // SB)
        c = {}
        for g in groups:
            blk = dz[g * SB : (g + 1) * SB, 0:NB]
            c[g] = [jnp.broadcast_to(blk[:, r0 + p : r0 + p + 1], (SB, NB)) for p in range(SB)]
        for p in range(SB):
            r = lax.rsqrt(e[p][p])
            rs[p] = rs[p] * r
            rw[p] = rw[p] * r
            f = {q: e[q][p] * r for q in range(p + 1, SB)}
            for q in range(p + 1, SB):
                for s in range(p + 1, q + 1):
                    e[q][s] = e[q][s] - f[q] * f[s]
            for q in range(p + 1, SB):
                rs[q] = rs[q] - f[q] * rs[p]
                rw[q] = rw[q] - f[q] * rw[p]
            for g in groups:
                c[g][p] = c[g][p] * r
                for q in range(p + 1, SB):
                    c[g][q] = c[g][q] - f[q] * c[g][p]
        for p in range(SB):
            vout[r0 + p : r0 + p + 1, :] = rw[p][0:1, :]
        for g in groups:
            ds = dz[g * SB : (g + 1) * SB, 0:NB]
            dw = dz[g * SB : (g + 1) * SB, NB : 2 * NB]
            for p in range(SB):
                ds = ds - c[g][p] * rs[p]
                dw = dw - c[g][p] * rw[p]
            dz[g * SB : (g + 1) * SB, 0:NB] = ds
            dz[g * SB : (g + 1) * SB, NB : 2 * NB] = dw


def inverse_factor(z, dz, vb, lhs, rhs):
    rows = lax.broadcasted_iota(jnp.int32, (NB, NB), 0)
    eye = jnp.where(rows == lax.broadcasted_iota(jnp.int32, (NB, NB), 1), 1.0, 0.0)
    zero = jnp.zeros((NB, NB), F32)

    def step(k, carry):
        ks = at(k, NB)
        dz[:, 0:NB] = z[ks, ks]
        dz[:, NB : 2 * NB] = eye
        diag_inverse(dz, vb)
        v = vb[...]
        vh, vm, vl = split3(v)
        zh, zm, zl = split3(z[ks, :])
        a = jnp.concatenate([vh, vh, vm, vh, vl, vm], axis=1)
        b = jnp.concatenate([zh, zm, zh, zl, zh, zm], axis=0)
        z[ks, :] = jnp.dot(a, b, preferred_element_type=F32)
        z[ks, ks] = v
        rh, rm, rl = split3(z[ks, :])
        for i, x in enumerate([rh, rm, rh, rl, rh, rm]):
            rhs[i * NB : (i + 1) * NB, :] = x
        for i, x in enumerate([rh, rh, rm, rh, rl, rm]):
            lhs[i * NB : (i + 1) * NB, :] = x

        def trail(i, carry):
            si = at(i, NB)
            z[si, ks] = zero
            z[si, :] = z[si, :] - lax.dot_general(lhs[:, si], rhs[...], TNDOT, preferred_element_type=F32)
            z[ks, si] = zero
            return carry

        return lax.fori_loop(k + 1, NK, trail, carry)

    lax.fori_loop(0, NK, step, 0)


def transform_kernel(scal, ga, gb, t_ref, corr_ref, z, dz, vb, lhs, rhs):
    core = scal[2]
    me = scal[0] * 4 + scal[1]
    rows = lax.broadcasted_iota(jnp.int32, (NB, NB), 0)
    ridge = jnp.where(rows == lax.broadcasted_iota(jnp.int32, (NB, NB), 1), N - 1.0, 0.0)
    half = (lax.broadcasted_iota(jnp.int32, (64, NB), 0) * 0 + core) == 0
    for i in range(NK):
        for d in range(NT):
            j = i + d
            if d == 4 and i >= 4:
                continue
            a = ga[i, 64 * d : 64 * d + 64, :]
            b = gb[i, 64 * d : 64 * d + 64, :]
            blk = jnp.concatenate([jnp.where(half, a, b), jnp.where(half, b, a)], axis=0)
            if d == 0:
                z[i * NB : (i + 1) * NB, i * NB : (i + 1) * NB] = blk + ridge
            elif j < NK:
                z[i * NB : (i + 1) * NB, j * NB : (j + 1) * NB] = blk
            else:
                z[(j - NK) * NB : (j - NK + 1) * NB, i * NB : (i + 1) * NB] = blk.T
    inverse_factor(z, dz, vb, lhs, rhs)
    drive = jnp.concatenate([ga[i, DRIVE : DRIVE + 1, :] for i in range(NK)], axis=1)

    def weigh(i, acc):
        x = z[at(i, 64), :]
        x = x * jnp.sum(x * drive, axis=1, keepdims=True)
        for q in range(8):
            acc = acc + x[q * 8 : (q + 1) * 8]
        return acc

    weights = jnp.sum(lax.fori_loop(0, N // 64, weigh, jnp.zeros((8, N), F32)), axis=0, keepdims=True)
    own = jnp.concatenate([z[at(2 * me + core, 64), :], z[at(2 * me + 1 - core, 64), :]], axis=0)
    t = (own * math.sqrt(N - 1) + weights).astype(BF)
    t_ref[...] = t
    corr_ref[...] = jnp.broadcast_to(1.0 - jnp.sum(t.astype(F32), axis=1, keepdims=True), corr_ref.shape)


def transform(scal, ga, gb):
    return pl.pallas_call(
        transform_kernel,
        out_shape=(jax.ShapeDtypeStruct((NB, N), BF), jax.ShapeDtypeStruct((NB, NB), F32)),
        in_specs=[SMEM, VMEM, VMEM],
        out_specs=(VMEM, VMEM),
        scratch_shapes=[
            pltpu.VMEM((N, N), F32),
            pltpu.VMEM((NB, 2 * NB), F32),
            pltpu.VMEM((NB, NB), F32),
            pltpu.VMEM((6 * NB, N), BF),
            pltpu.VMEM((6 * NB, N), BF),
        ],
        compiler_params=params(40),
        cost_estimate=pl.CostEstimate(flops=10**10, bytes_accessed=4 * 2**20, transcendentals=0),
        name="transform",
    )(scal, ga, gb)


def update_kernel(scal, t_ref, corr_ref, mean_ref, *refs):
    pieces = refs[:8]
    keep, send = refs[8:]
    corr = corr_ref[:, 0:1]
    acc = corr * mean_ref[0:1, :]
    for p, (sx, sy) in zip(pieces, SHIFTS):
        acc = acc + jnp.dot(t_ref[:, at(chip_of(scal, sx, sy), NB)], p[...], preferred_element_type=F32)
    keep[...] = acc[:64].astype(BF)
    send[...] = acc[64:].astype(BF)


def update(scal, t, corr, mean, pieces):
    part = jax.ShapeDtypeStruct((64, HALF), BF)
    return pl.pallas_call(
        update_kernel,
        out_shape=(part, part),
        in_specs=[SMEM] + [VMEM] * 11,
        out_specs=(VMEM, VMEM),
        compiler_params=params(32),
        cost_estimate=pl.CostEstimate(flops=2 * NB * N * HALF, bytes_accessed=5 * 2**20, transcendentals=0),
        name="update",
    )(scal, t, corr, mean, *pieces)


def swap(x):
    return lax.ppermute(x, "core", [(0, 1), (1, 0)])


def from_chip(x, sx, sy):
    if sx + sy == 0:
        return x
    pairs = [(y * 4 + i, ((y + sy) % 2) * 4 + (i + sx) % 4) for y in range(2) for i in range(4)]
    return lax.ppermute(x, ("yh", "x"), pairs)


def gather(x, axes, size):
    return lax.all_to_all(jnp.broadcast_to(x[None], (size, *x.shape)), axes, 0, 0, tiled=True)


def per_device(background_samples, sensor_cell_offsets, sensor_data, sensor_sigma_list):
    core = lax.axis_index("core")
    scal = jnp.stack([lax.axis_index("yh"), lax.axis_index("x"), core]).astype(jnp.int32)
    low, high = background_samples[:, :HALF], background_samples[:, HALF:]
    first = core == 0
    mine = jnp.where(first, low, high)
    got = swap(jnp.where(first, high, low))
    block = jnp.where(first, jnp.concatenate([mine, got]), jnp.concatenate([got, mine]))
    pieces = [from_chip(block, sx, sy) for sx, sy in SHIFTS]
    ws = obs_sums(scal, sensor_cell_offsets, sensor_data, sensor_sigma_list)
    keep, send, mean = gram_part(scal, ws, pieces)
    part = keep + swap(send)
    part = lax.all_to_all(part.reshape(16, 24, NB), ("z", "yl"), 0, 0, tiled=True)
    part = gather(jnp.sum(part, axis=0), ("z", "yl"), 16).reshape(ROWS, NB)
    ga = gather(part, ("yh", "x"), 8)
    gb = swap(ga)
    t, corr = transform(scal, ga, gb)
    keep, send = update(scal, t, corr, mean, pieces)
    got = swap(send)
    return jnp.where(first, jnp.concatenate([keep, got], axis=1), jnp.concatenate([got, keep], axis=1))


def solution(mesh):
    names = ("yh", "x", "core", "z", "yl")
    split = Mesh(mesh.devices.reshape(2, 4, 2, 8, 2), names)
    mem, sp = names[:3], names[3:]
    return jax.shard_map(
        per_device,
        mesh=split,
        in_specs=(P(mem, sp), P(sp), P(sp), P(sp)),
        out_specs=P(mem, sp),
        check_vma=False,
    )
```

time: 872 us -> 199 us (0.23)
  other arithmetic: 269 us -> 2.23 us
  waiting for transfers between devices: 243 us -> 42.5 us
  local copies, waits for them, and re-layouts: 119 us -> 0.13 us
  blocking collectives: 143 us -> 60.3 us
  matrix products: 70.2 us -> 0 us
  Pallas kernels: 0 us -> 55.8 us
  starting transfers between devices: 0.12 us -> 37.9 us
  between operations: 19.9 us -> 0.09 us
    another operation x33 -> x1, other arithmetic: 251 us -> 0.08 us  [per_device(): jnp.stack([lax.axis_index('yh'), lax.axis_index('x'), core])]
    psum x1 -> x0, waiting for transfers between devices: 123 us -> none  [per_device(): gram_cols, drive_cols = lax.psum((gram_cols, drive_cols), 'sp')]
    all_gather x3 -> x0, waiting for transfers between devices: 120 us -> none  [the longest x1 120 us: per_device(): lax.all_gather(scaled, 'mem', axis=0, tiled=True)]
    psum x2 -> x0, blocking collectives: 91.6 us -> none  [the longest x1 65.2 us: per_device(): predicted_centroid = lax.psum(running_block_tally, 'mem') / sample_cloud]
    gather x2 -> x0, local copies, waits for them, and re-layouts: 74.8 us -> none  [the longest x1 45.5 us: per_device(): jnp.take(predicted_centroid, sensor_cell_offsets)]
    all_to_all x0 -> x3, blocking collectives: none -> 60.3 us  [the longest x2 39 us: gather(): lax.all_to_all(jnp.broadcast_to(x[None], (size, *x.shape)), axes, 0, 0, t...]
    pallas_call x0 -> x4, Pallas kernels: none -> 55.8 us  [the longest x1 47.2 us: transform(): pl.pallas_call(transform_kernel, out_shape=(jax.ShapeDtypeStruct((NB, N),...]
    another operation x59 -> x0, matrix products: 51.5 us -> none  [the longest x14 27 us: per_device(): factor = jnp.linalg.cholesky(gram_matrix)]
  transfers between devices with their start and end apart: 4 -> 11, of which waited for: 2 -> 9; matrix products, arithmetic and copies ran while one was open for 41% -> 0% of each run, Pallas kernels for 0% -> 1%
where the time goes in v1:
time: 199 us
  blocking collectives  60.3 us (30%)
  Pallas kernels  55.8 us (28%)
  waiting for transfers between devices  42.5 us (21%)
  starting transfers between devices  37.9 us (19%)
  other arithmetic  2.23 us (1%)
    pallas_call x1, Pallas kernels, transform(): pl.pallas_call(transform_kernel, out_shape=(jax.ShapeDtypeStruct((NB, N),...  47.2 us
    all_to_all x2, blocking collectives, gather(): lax.all_to_all(jnp.broadcast_to(x[None], (size, *x.shape)), axes, 0, 0, t...  39 us
    ppermute x7, waiting for transfers between devices, from_chip(): return lax.ppermute(x, ('yh', 'x'), pairs)  36.1 us
    ppermute x7, starting transfers between devices, from_chip(): return lax.ppermute(x, ('yh', 'x'), pairs)  29 us
    all_to_all x1, blocking collectives, per_device(): lax.all_to_all(part.reshape(16, 24, NB), ('z', 'yl'), 0, 0, tiled=True)  21.3 us
    ppermute x4, starting transfers between devices, swap(): return lax.ppermute(x, 'core', [(0, 1), (1, 0)])  8.89 us
    ppermute x4, waiting for transfers between devices, swap(): return lax.ppermute(x, 'core', [(0, 1), (1, 0)])  6.43 us
    pallas_call x1, Pallas kernels, gram_part(): pl.pallas_call(gram_kernel, out_shape=(part, part, jax.ShapeDtypeStruct((...  4.04 us
  transfers between devices with their start and end apart: 11, of which 9 were waited for; matrix products, arithmetic and copies ran while one was open for 0% of the time, Pallas kernels for 1%

profile of v1, /device:TPU:1, one launch (start us, length us, event | category | flops | bytes accessed | tf_op | source)
XLA Modules:
  0.0 199.1 jit_solution(15366071472199457580)
XLA Ops:
  0.0 1.1 broadcast_select_fusion.1
  1.1 3.3 %collective-permute-start = (bf16[64,2048]{1,0:T(8,128)(2,1)S(1)}, bf16[64,2048]{1,0:T(8,128)(2,1)S(1)}, u32[]{:S(2)}, u32[]{:S(2)}) collective-permute-start(bf16[64,2048]{1,0:T(8,128)(2,1)S(1)} %get-tuple-element.20), channel_id=1, source_target_pairs={{0,16},{16,0},{1,17},{17,1},{2,18},{18,2},{3,19},{19,3},{4,20},{20... | collective-permute-start | bytes 786440 | tf_op jit(solution)/shard_map/ppermute | solution.py:295
  4.4 1.2 collective-permute-done
  5.6 0.1 maximum_select_fusion.refs_0_
  5.7 3.5 %collective-permute-start.7 = (bf16[128,2048]{1,0:T(8,128)(2,1)S(1)}, bf16[128,2048]{1,0:T(8,128)(2,1)S(1)}, u32[]{:S(2)}, u32[]{:S(2)}) collective-permute-start(bf16[128,2048]{1,0:T(8,128)(2,1)S(1)} %maximum_select_fusion.refs_0_), channel_id=1, source_target_pairs={{0,224},{32,128},{64,160},{96,192},{128,96},{160,0},{192,32},{224,... | collective-permute-start | bytes 1572872 | tf_op jit(solution)/shard_map/ppermute | solution.py:302
  9.2 0.4 collective-permute-start.6
  9.5 3.2 %collective-permute-start.5 = (bf16[128,2048]{1,0:T(8,128)(2,1)S(1)}, bf16[128,2048]{1,0:T(8,128)(2,1)S(1)}, u32[]{:S(2)}, u32[]{:S(2)}) collective-permute-start(bf16[128,2048]{1,0:T(8,128)(2,1)S(1)} %maximum_select_fusion.refs_0_), channel_id=1, source_target_pairs={{0,160},{32,192},{64,224},{96,128},{128,32},{160,64},{192,96},{224... | collective-permute-start | bytes 1572872 | tf_op jit(solution)/shard_map/ppermute | solution.py:302
  12.7 0.1 collective-permute-start.4
  12.8 2.1 %collective-permute-start.3 = (bf16[128,2048]{1,0:T(8,128)(2,1)S(1)}, bf16[128,2048]{1,0:T(8,128)(2,1)S(1)}, u32[]{:S(2)}, u32[]{:S(2)}) collective-permute-start(bf16[128,2048]{1,0:T(8,128)(2,1)S(1)} %maximum_select_fusion.refs_0_), channel_id=1, source_target_pairs={{0,96},{32,0},{64,32},{96,64},{128,224},{160,128},{192,160},{224,1... | collective-permute-start | bytes 1572872 | tf_op jit(solution)/shard_map/ppermute | solution.py:302
  14.9 15.0 %collective-permute-done.7.refs_7_ = bf16[128,2048]{1,0:T(8,128)(2,1)S(1)} collective-permute-done((bf16[128,2048]{1,0:T(8,128)(2,1)S(1)}, bf16[128,2048]{1,0:T(8,128)(2,1)S(1)}, u32[]{:S(2)}, u32[]{:S(2)}) %collective-permute-start.7) | collective-permute-done | bytes 524320 | tf_op jit(solution)/shard_map/ppermute | solution.py:302
  29.9 4.8 %collective-permute-start.2 = (bf16[128,2048]{1,0:T(8,128)(2,1)S(1)}, bf16[128,2048]{1,0:T(8,128)(2,1)}, u32[]{:S(2)}, u32[]{:S(2)}) collective-permute-start(bf16[128,2048]{1,0:T(8,128)(2,1)S(1)} %maximum_select_fusion.refs_0_), channel_id=1, source_target_pairs={{0,64},{32,96},{64,0},{96,32},{128,192},{160,224},{192,128},{224,1... | collective-permute-start | bytes 1572872 | tf_op jit(solution)/shard_map/ppermute | solution.py:302
  34.8 15.0 %collective-permute-start.1 = (bf16[128,2048]{1,0:T(8,128)(2,1)S(1)}, bf16[128,2048]{1,0:T(8,128)(2,1)}, u32[]{:S(2)}, u32[]{:S(2)}) collective-permute-start(bf16[128,2048]{1,0:T(8,128)(2,1)S(1)} %maximum_select_fusion.refs_0_), channel_id=1, source_target_pairs={{0,32},{32,64},{64,96},{96,0},{128,160},{160,192},{192,224},{224,1... | collective-permute-start | bytes 1572872 | tf_op jit(solution)/shard_map/ppermute | solution.py:302
  49.8 0.1 pad_add_fusion.scal
  49.8 2.1 %obs_sums.1.ws_ref = f32[8,2048]{1,0:T(8,128)S(1)} custom-call(s32[3]{0:T(128)S(1)} %pad_add_fusion.scal, s32[64,128]{1,0:T(8,128)S(1)} %bitcast.8, f32[64,128]{1,0:T(8,128)S(1)} %bitcast.9, f32[64,128]{1,0:T(8,128)S(1)} %bitcast.10), custom_call_target="tpu_custom_call" | custom-call | flops 201326592 | bytes 200000 | tf_op jit(solution)/shard_map/obs_sums/pallas_call | solution.py:69
  52.0 3.8 %collective-permute-done.4.refs_4_ = bf16[128,2048]{1,0:T(8,128)(2,1)S(1)} collective-permute-done((bf16[128,2048]{1,0:T(8,128)(2,1)S(1)}, bf16[128,2048]{1,0:T(8,128)(2,1)S(1)}, u32[]{:S(2)}, u32[]{:S(2)}) %collective-permute-start.4) | collective-permute-done | bytes 524320 | tf_op jit(solution)/shard_map/ppermute | solution.py:302
  55.8 0.5 collective-permute-done.3.refs_3_
  56.4 4.5 %collective-permute-done.2.refs_2_ = bf16[128,2048]{1,0:T(8,128)(2,1)} collective-permute-done((bf16[128,2048]{1,0:T(8,128)(2,1)S(1)}, bf16[128,2048]{1,0:T(8,128)(2,1)}, u32[]{:S(2)}, u32[]{:S(2)}) %collective-permute-start.2) | collective-permute-done | bytes 524320 | tf_op jit(solution)/shard_map/ppermute | solution.py:302
  60.8 12.2 %collective-permute-done.1.refs_1_ = bf16[128,2048]{1,0:T(8,128)(2,1)} collective-permute-done((bf16[128,2048]{1,0:T(8,128)(2,1)S(1)}, bf16[128,2048]{1,0:T(8,128)(2,1)}, u32[]{:S(2)}, u32[]{:S(2)}) %collective-permute-start.1) | collective-permute-done | bytes 524320 | tf_op jit(solution)/shard_map/ppermute | solution.py:302
  73.1 4.0 %gram_part.1 = (f32[384,128]{1,0:T(8,128)S(1)}, f32[384,128]{1,0:T(8,128)S(1)}, f32[8,2048]{1,0:T(8,128)S(1)}) custom-call(s32[3]{0:T(128)S(1)} %pad_add_fusion.scal, f32[8,2048]{1,0:T(8,128)S(1)} %obs_sums.1.ws_ref, bf16[128,2048]{1,0:T(8,128)(2,1)S(1)} %maximum_select_fusion.refs_0_, bf16[128,2048]{1,0:T(8,128)(2,1)} %collective-permute-done.1.refs_1_, ...), custom_call_target="tpu_custom_call" | custom-call | flops 335544320 | bytes 5242880 | tf_op jit(solution)/shard_map/gram_part/pallas_call | solution.py:129
  77.1 0.6 collective-permute-start.8
  77.7 1.1 collective-permute-done.8
  78.8 21.3 %all_to_all.15 = f32[16,24,128]{2,1,0:T(8,128)S(1)} all-to-all(f32[16,24,128]{2,1,0:T(8,128)S(1)} %bitcast.12), channel_id=1, replica_groups=mesh['yh'=2,'x'=4,'core'=2,'z'=8,'yl'=2] {'z','yl'}, dimensions={0} | all-to-all | bytes 393216 | tf_op jit(solution)/shard_map/all_to_all | solution.py:321
  100.2 11.9 %all_to_all.16 = f32[16,24,128]{2,1,0:T(8,128)S(1)} all-to-all(f32[16,24,128]{2,1,0:T(8,128)S(1)} %broadcast_in_dim.6), channel_id=1, replica_groups=mesh['yh'=2,'x'=4,'core'=2,'z'=8,'yl'=2] {'z','yl'}, dimensions={0} | all-to-all | bytes 393216 | tf_op jit(solution)/shard_map/all_to_all | solution.py:306
  112.0 0.1 broadcast_in_dim.15
  112.1 27.2 %all_to_all.17.ga = f32[8,384,128]{2,1,0:T(8,128)S(1)} all-to-all(f32[8,384,128]{2,1,0:T(8,128)S(1)} %broadcast_in_dim.15), channel_id=1, replica_groups=mesh['yh'=2,'x'=4,'core'=2,'z'=8,'yl'=2] {'yh','x'}, dimensions={0} | all-to-all | bytes 3145728 | tf_op jit(solution)/shard_map/all_to_all | solution.py:306
  139.3 4.5 %collective-permute-start.9 = (f32[8,384,128]{2,1,0:T(8,128)S(1)}, f32[8,384,128]{2,1,0:T(8,128)S(1)}, u32[]{:S(2)}, u32[]{:S(2)}) collective-permute-start(f32[8,384,128]{2,1,0:T(8,128)S(1)} %all_to_all.17.ga), channel_id=1, source_target_pairs={{0,16},{16,0},{1,17},{17,1},{2,18},{18,2},{3,19},{19,3},{4,20},{20... | collective-permute-start | bytes 4718600 | tf_op jit(solution)/shard_map/ppermute | solution.py:295
  143.8 3.0 %collective-permute-done.9.gb = f32[8,384,128]{2,1,0:T(8,128)S(1)} collective-permute-done((f32[8,384,128]{2,1,0:T(8,128)S(1)}, f32[8,384,128]{2,1,0:T(8,128)S(1)}, u32[]{:S(2)}, u32[]{:S(2)}) %collective-permute-start.9) | collective-permute-done | bytes 1572896 | tf_op jit(solution)/shard_map/ppermute | solution.py:295
  146.9 47.2 %transform.1 = (bf16[128,1024]{1,0:T(8,128)(2,1)S(1)}, f32[128,128]{1,0:T(8,128)S(1)}) custom-call(s32[3]{0:T(128)S(1)} %pad_add_fusion.scal, f32[8,384,128]{2,1,0:T(8,128)S(1)} %all_to_all.17.ga, f32[8,384,128]{2,1,0:T(8,128)S(1)} %collective-permute-done.9.gb), custom_call_target="tpu_custom_call" | custom-call | flops 10000000000 | bytes 4194304 | tf_op jit(solution)/shard_map/transform/pallas_call | solution.py:252
  194.1 2.4 %update.1 = (bf16[64,2048]{1,0:T(8,128)(2,1)S(1)}, bf16[64,2048]{1,0:T(8,128)(2,1)S(1)}) custom-call(s32[3]{0:T(128)S(1)} %pad_add_fusion.scal, bf16[128,1024]{1,0:T(8,128)(2,1)S(1)} %get-tuple-element.14.t_ref, f32[128,128]{1,0:T(8,128)S(1)} %get-tuple-element.15.corr_ref, f32[8,2048]{1,0:T(8,128)S(1)} %get-tuple-element.16.mean_ref, ...), custom_call_target="tpu_custom_call" | custom-call | flops 536870912 | bytes 5242880 | tf_op jit(solution)/shard_map/update/pallas_call | solution.py:283
  196.5 0.5 collective-permute-start.10
  197.0 1.2 collective-permute-done.10
  198.2 0.9 maximum_select_fusion.1
  (11 shorter events, 0.1 us)
Async XLA Ops:
  0.0 49.8 %copy-start.2 = (f32[8192]{0:T(1024)S(1)}, f32[8192]{0:T(1024)}, u32[]{:S(2)}) copy-start(f32[8192]{0:T(1024)} %param.7) | copy-start | bytes 98308
  0.0 49.8 %copy-start.1 = (f32[8192]{0:T(1024)S(1)}, f32[8192]{0:T(1024)}, u32[]{:S(2)}) copy-start(f32[8192]{0:T(1024)} %param.6) | copy-start | bytes 98308
  0.0 49.8 %copy-start = (s32[8192]{0:T(1024)S(1)}, s32[8192]{0:T(1024)}, u32[]{:S(2)}) copy-start(s32[8192]{0:T(1024)} %param.5) | copy-start | bytes 98308
  1.1 4.5 %collective-permute-start = (bf16[64,2048]{1,0:T(8,128)(2,1)S(1)}, bf16[64,2048]{1,0:T(8,128)(2,1)S(1)}, u32[]{:S(2)}, u32[]{:S(2)}) collective-permute-start(bf16[64,2048]{1,0:T(8,128)(2,1)S(1)} %get-tuple-element.20), channel_id=1, source_target_pairs={{0,16},{16,0},{1,17},{17,1},{2,18},{18,2},{3,19},{19,3},{4,20},{20... | collective-permute-start | bytes 786440 | tf_op jit(solution)/shard_map/ppermute | solution.py:295
  5.7 24.2 %collective-permute-start.7 = (bf16[128,2048]{1,0:T(8,128)(2,1)S(1)}, bf16[128,2048]{1,0:T(8,128)(2,1)S(1)}, u32[]{:S(2)}, u32[]{:S(2)}) collective-permute-start(bf16[128,2048]{1,0:T(8,128)(2,1)S(1)} %maximum_select_fusion.refs_0_), channel_id=1, source_target_pairs={{0,224},{32,128},{64,160},{96,192},{128,96},{160,0},{192,32},{224,... | collective-permute-start | bytes 1572872 | tf_op jit(solution)/shard_map/ppermute | solution.py:302
  9.2 25.6 %collective-permute-start.6 = (bf16[128,2048]{1,0:T(8,128)(2,1)S(1)}, bf16[128,2048]{1,0:T(8,128)(2,1)S(1)}, u32[]{:S(2)}, u32[]{:S(2)}) collective-permute-start(bf16[128,2048]{1,0:T(8,128)(2,1)S(1)} %maximum_select_fusion.refs_0_), channel_id=1, source_target_pairs={{0,192},{32,224},{64,128},{96,160},{128,64},{160,96},{192,0},{224,... | collective-permute-start | bytes 1572872 | tf_op jit(solution)/shard_map/ppermute | solution.py:302
  9.5 42.4 %collective-permute-start.5 = (bf16[128,2048]{1,0:T(8,128)(2,1)S(1)}, bf16[128,2048]{1,0:T(8,128)(2,1)S(1)}, u32[]{:S(2)}, u32[]{:S(2)}) collective-permute-start(bf16[128,2048]{1,0:T(8,128)(2,1)S(1)} %maximum_select_fusion.refs_0_), channel_id=1, source_target_pairs={{0,160},{32,192},{64,224},{96,128},{128,32},{160,64},{192,96},{224... | collective-permute-start | bytes 1572872 | tf_op jit(solution)/shard_map/ppermute | solution.py:302
  12.7 43.1 %collective-permute-start.4 = (bf16[128,2048]{1,0:T(8,128)(2,1)S(1)}, bf16[128,2048]{1,0:T(8,128)(2,1)S(1)}, u32[]{:S(2)}, u32[]{:S(2)}) collective-permute-start(bf16[128,2048]{1,0:T(8,128)(2,1)S(1)} %maximum_select_fusion.refs_0_), channel_id=1, source_target_pairs={{0,128},{32,160},{64,192},{96,224},{128,0},{160,32},{192,64},{224,... | collective-permute-start | bytes 1572872 | tf_op jit(solution)/shard_map/ppermute | solution.py:302
  12.8 43.6 %collective-permute-start.3 = (bf16[128,2048]{1,0:T(8,128)(2,1)S(1)}, bf16[128,2048]{1,0:T(8,128)(2,1)S(1)}, u32[]{:S(2)}, u32[]{:S(2)}) collective-permute-start(bf16[128,2048]{1,0:T(8,128)(2,1)S(1)} %maximum_select_fusion.refs_0_), channel_id=1, source_target_pairs={{0,96},{32,0},{64,32},{96,64},{128,224},{160,128},{192,160},{224,1... | collective-permute-start | bytes 1572872 | tf_op jit(solution)/shard_map/ppermute | solution.py:302
  29.9 30.9 %collective-permute-start.2 = (bf16[128,2048]{1,0:T(8,128)(2,1)S(1)}, bf16[128,2048]{1,0:T(8,128)(2,1)}, u32[]{:S(2)}, u32[]{:S(2)}) collective-permute-start(bf16[128,2048]{1,0:T(8,128)(2,1)S(1)} %maximum_select_fusion.refs_0_), channel_id=1, source_target_pairs={{0,64},{32,96},{64,0},{96,32},{128,192},{160,224},{192,128},{224,1... | collective-permute-start | bytes 1572872 | tf_op jit(solution)/shard_map/ppermute | solution.py:302
  34.8 38.3 %collective-permute-start.1 = (bf16[128,2048]{1,0:T(8,128)(2,1)S(1)}, bf16[128,2048]{1,0:T(8,128)(2,1)}, u32[]{:S(2)}, u32[]{:S(2)}) collective-permute-start(bf16[128,2048]{1,0:T(8,128)(2,1)S(1)} %maximum_select_fusion.refs_0_), channel_id=1, source_target_pairs={{0,32},{32,64},{64,96},{96,0},{128,160},{160,192},{192,224},{224,1... | collective-permute-start | bytes 1572872 | tf_op jit(solution)/shard_map/ppermute | solution.py:302
  77.1 1.7 collective-permute-start.8
  139.3 7.6 %collective-permute-start.9 = (f32[8,384,128]{2,1,0:T(8,128)S(1)}, f32[8,384,128]{2,1,0:T(8,128)S(1)}, u32[]{:S(2)}, u32[]{:S(2)}) collective-permute-start(f32[8,384,128]{2,1,0:T(8,128)S(1)} %all_to_all.17.ga), channel_id=1, source_target_pairs={{0,16},{16,0},{1,17},{17,1},{2,18},{18,2},{3,19},{19,3},{4,20},{20... | collective-permute-start | bytes 4718600 | tf_op jit(solution)/shard_map/ppermute | solution.py:295
  196.5 1.6 collective-permute-start.10

commit v2 on v1

v2 whole, which is shorter than its diff:
```python
import math

import jax
import jax.numpy as jnp
from jax import lax
from jax.experimental import pallas as pl
from jax.experimental.pallas import tpu as pltpu
from jax.sharding import Mesh, PartitionSpec as P

F32 = jnp.float32
BF = jnp.bfloat16
N = 1024
CELLS = 4096
OBS = 8192
HALF = CELLS // 2
NB = 128
SB = 8
NK = N // NB
PART = CELLS // NK
PART_HI = PART // NB
GROWS = 144
VMEM = pl.BlockSpec(memory_space=pltpu.VMEM)
SMEM = pl.BlockSpec(memory_space=pltpu.SMEM)
NTDOT = (((1,), (1,)), ((), ()))
TNDOT = (((0,), (0,)), ((), ()))


def params(mib):
    return pltpu.CompilerParams(vmem_limit_bytes=mib * 2**20)


def split3(x):
    h = x.astype(BF)
    r = x - h.astype(F32)
    m = r.astype(BF)
    return h, m, (r - m.astype(F32)).astype(BF)


def at(i, size):
    return pl.ds(pl.multiple_of(i * size, size), size)


def obs_kernel(scal, off_ref, data_ref, sigma_ref, out_ref, lhs, oh):
    first = (scal[0] * 4 + scal[1]) * PART_HI
    row = lax.broadcasted_iota(jnp.int32, (8, NB), 0)
    hi_iota = (row & 3) + first
    lower = row < 4
    lo_iota = lax.broadcasted_iota(jnp.int32, (NB, NB), 0)
    for r in range(OBS // NB):
        off = off_ref[r : r + 1, :]
        sigma = sigma_ref[r : r + 1, :]
        w = 1.0 / (sigma * sigma)
        s = data_ref[r : r + 1, :] * w
        mask = lax.shift_right_logical(off, 7) == hi_iota
        cols = slice(r * NB, (r + 1) * NB)
        v = [x.astype(F32) for x in split3(w) + split3(s)]
        blocks = [jnp.where(mask, jnp.where(lower, v[2 * i], v[2 * i + 1]), 0.0) for i in range(3)]
        lhs[:, cols] = jnp.concatenate(blocks + [jnp.zeros((8, NB), F32)], axis=0).astype(BF)
        oh[:, cols] = jnp.where((off & 127) == lo_iota, 1.0, 0.0).astype(BF)
    t = lax.dot_general(lhs[...], oh[...], NTDOT, preferred_element_type=F32)
    w = t[0:4] + t[4:8] + t[8:12]
    s = t[12:16] + t[16:20] + t[20:24]
    out_ref[...] = jnp.zeros_like(out_ref)
    for h in range(PART_HI):
        out_ref[0:1, h * NB : (h + 1) * NB] = w[h : h + 1]
        out_ref[1:2, h * NB : (h + 1) * NB] = s[h : h + 1]


def obs_sums(scal, off, data, sigma):
    shape = (OBS // NB, NB)
    return pl.pallas_call(
        obs_kernel,
        out_shape=jax.ShapeDtypeStruct((8, PART), F32),
        in_specs=[SMEM, VMEM, VMEM, VMEM],
        out_specs=VMEM,
        scratch_shapes=[pltpu.VMEM((32, OBS), BF), pltpu.VMEM((NB, OBS), BF)],
        compiler_params=params(24),
        cost_estimate=pl.CostEstimate(flops=2 * 32 * NB * OBS, bytes_accessed=200000, transcendentals=0),
        name="obs_sums",
    )(scal, off.reshape(shape), data.reshape(shape), sigma.reshape(shape))


def blocks_of(core):
    return [(4 * core + i, d) for d in range(4) for i in range(4)] + [(2 * core + i, 4) for i in range(2)]


def gram_kernel(scal, ws_ref, xa, xb, out_ref, b):
    core = scal[2]
    total = jnp.zeros((1, PART), F32)
    for i in range(NK):
        total = total + jnp.sum(xa[i].astype(F32), axis=0, keepdims=True) + jnp.sum(xb[i].astype(F32), axis=0, keepdims=True)
    mean = total * (1.0 / N)
    w = ws_ref[0:1, :]
    root = jnp.sqrt(w)
    for i in range(NK):
        b[at(2 * i + core, 64), :] = ((xa[i].astype(F32) - mean) * root).astype(BF)
        b[at(2 * i + 1 - core, 64), :] = ((xb[i].astype(F32) - mean) * root).astype(BF)
    d = jnp.where(w > 0.0, (ws_ref[1:2, :] - mean * w) * lax.rsqrt(jnp.where(w > 0.0, w, 1.0)), 0.0)
    d = jnp.concatenate([x.astype(F32) for x in split3(d)] + [jnp.zeros((13, PART), F32)], axis=0).astype(BF)
    drive = lax.dot_general(d, b[...], NTDOT, preferred_element_type=F32)
    drive = jnp.sum(drive, axis=0, keepdims=True)
    drive = jnp.concatenate([drive[:, i * NB : (i + 1) * NB] for i in range(NK)], axis=0)
    for t in range(16):
        out_ref[t, GROWS:, :] = drive
    for n, (i, d) in enumerate(blocks_of(0)):
        i = i + core * (4 if d < 4 else 2)
        g = lax.dot_general(b[at(i, NB), :], b[at((i + d) % NK, NB), :], NTDOT, preferred_element_type=F32)
        row = 0
        while row < NB:
            t, r = divmod(n * NB + row, GROWS)
            size = min(NB - row, GROWS - r)
            out_ref[t, r : r + size, :] = g[row : row + size]
            row += size


def gram_part(scal, ws, xa, xb):
    return pl.pallas_call(
        gram_kernel,
        out_shape=jax.ShapeDtypeStruct((16, GROWS + 8, NB), F32),
        in_specs=[SMEM] + [VMEM] * 3,
        out_specs=VMEM,
        scratch_shapes=[pltpu.VMEM((N, PART), BF)],
        compiler_params=params(32),
        cost_estimate=pl.CostEstimate(flops=2 * NB * NB * 18 * PART, bytes_accessed=3 * 2**20, transcendentals=0),
        name="gram_part",
    )(scal, ws, xa, xb)


def diag_inverse(dz, vout):
    for j in range(NB // SB):
        r0 = j * SB
        rs = [jnp.broadcast_to(dz[r0 + p : r0 + p + 1, 0:NB], (SB, NB)) for p in range(SB)]
        rw = [jnp.broadcast_to(dz[r0 + p : r0 + p + 1, NB : 2 * NB], (SB, NB)) for p in range(SB)]
        e = [[jnp.broadcast_to(rs[q][:, r0 + p : r0 + p + 1], (SB, NB)) for p in range(q + 1)] for q in range(SB)]
        groups = range(j + 1, NB // SB)
        c = {}
        for g in groups:
            blk = dz[g * SB : (g + 1) * SB, 0:NB]
            c[g] = [jnp.broadcast_to(blk[:, r0 + p : r0 + p + 1], (SB, NB)) for p in range(SB)]
        for p in range(SB):
            r = lax.rsqrt(e[p][p])
            rs[p] = rs[p] * r
            rw[p] = rw[p] * r
            f = {q: e[q][p] * r for q in range(p + 1, SB)}
            for q in range(p + 1, SB):
                for s in range(p + 1, q + 1):
                    e[q][s] = e[q][s] - f[q] * f[s]
            for q in range(p + 1, SB):
                rs[q] = rs[q] - f[q] * rs[p]
                rw[q] = rw[q] - f[q] * rw[p]
            for g in groups:
                c[g][p] = c[g][p] * r
                for q in range(p + 1, SB):
                    c[g][q] = c[g][q] - f[q] * c[g][p]
        for p in range(SB):
            vout[r0 + p : r0 + p + 1, :] = rw[p][0:1, :]
        for g in groups:
            ds = dz[g * SB : (g + 1) * SB, 0:NB]
            dw = dz[g * SB : (g + 1) * SB, NB : 2 * NB]
            for p in range(SB):
                ds = ds - c[g][p] * rs[p]
                dw = dw - c[g][p] * rw[p]
            dz[g * SB : (g + 1) * SB, 0:NB] = ds
            dz[g * SB : (g + 1) * SB, NB : 2 * NB] = dw


def inverse_factor(z, dz, vb, lhs, rhs):
    rows = lax.broadcasted_iota(jnp.int32, (NB, NB), 0)
    eye = jnp.where(rows == lax.broadcasted_iota(jnp.int32, (NB, NB), 1), 1.0, 0.0)
    zero = jnp.zeros((NB, NB), F32)

    def step(k, carry):
        ks = at(k, NB)
        dz[:, 0:NB] = z[ks, ks]
        dz[:, NB : 2 * NB] = eye
        diag_inverse(dz, vb)
        v = vb[...]
        vh, vm, vl = split3(v)
        zh, zm, zl = split3(z[ks, :])
        a = jnp.concatenate([vh, vh, vm, vh, vl, vm], axis=1)
        b = jnp.concatenate([zh, zm, zh, zl, zh, zm], axis=0)
        z[ks, :] = jnp.dot(a, b, preferred_element_type=F32)
        z[ks, ks] = v
        rh, rm, rl = split3(z[ks, :])
        for i, x in enumerate([rh, rm, rh, rl, rh, rm]):
            rhs[i * NB : (i + 1) * NB, :] = x
        for i, x in enumerate([rh, rh, rm, rh, rl, rm]):
            lhs[i * NB : (i + 1) * NB, :] = x

        def trail(i, carry):
            si = at(i, NB)
            z[si, ks] = zero
            z[si, :] = z[si, :] - lax.dot_general(lhs[:, si], rhs[...], TNDOT, preferred_element_type=F32)
            z[ks, si] = zero
            return carry

        return lax.fori_loop(k + 1, NK, trail, carry)

    lax.fori_loop(0, NK, step, 0)


def transform_kernel(scal, ga, gb, drive_ref, t_ref, corr_ref, z, dz, vb, lhs, rhs):
    core = scal[2]
    me = scal[0] * 4 + scal[1]
    rows = lax.broadcasted_iota(jnp.int32, (NB, NB), 0)
    ridge = jnp.where(rows == lax.broadcasted_iota(jnp.int32, (NB, NB), 1), N - 1.0, 0.0)
    zero_core = (rows * 0 + core) == 0
    for c in range(2):
        for n, (i, d) in enumerate(blocks_of(c)):
            j = i + d
            a = ga[n * NB : (n + 1) * NB, :]
            b = gb[n * NB : (n + 1) * NB, :]
            blk = jnp.where(zero_core, a, b) if c == 0 else jnp.where(zero_core, b, a)
            if d == 0:
                z[i * NB : (i + 1) * NB, i * NB : (i + 1) * NB] = blk + ridge
            elif j < NK:
                z[i * NB : (i + 1) * NB, j * NB : (j + 1) * NB] = blk
            else:
                z[(j - NK) * NB : (j - NK + 1) * NB, i * NB : (i + 1) * NB] = blk.T
    inverse_factor(z, dz, vb, lhs, rhs)
    drive = jnp.concatenate([drive_ref[i : i + 1, :] for i in range(NK)], axis=1)

    def weigh(i, acc):
        x = z[at(i, 64), :]
        x = x * jnp.sum(x * drive, axis=1, keepdims=True)
        for q in range(8):
            acc = acc + x[q * 8 : (q + 1) * 8]
        return acc

    weights = jnp.sum(lax.fori_loop(0, N // 64, weigh, jnp.zeros((8, N), F32)), axis=0, keepdims=True)
    own = jnp.concatenate([z[at(2 * me + core, 64), :], z[at(2 * me + 1 - core, 64), :]], axis=0)
    t = (own * math.sqrt(N - 1) + weights).astype(BF)
    t_ref[0:NB, :] = t
    t_ref[NB:, :] = jnp.full((16, N), 1.0 / N, BF)
    corr_ref[...] = jnp.broadcast_to(1.0 - jnp.sum(t.astype(F32), axis=1, keepdims=True), corr_ref.shape)


def transform(scal, ga, gb, drive):
    return pl.pallas_call(
        transform_kernel,
        out_shape=(jax.ShapeDtypeStruct((NB + 16, N), BF), jax.ShapeDtypeStruct((NB, NB), F32)),
        in_specs=[SMEM, VMEM, VMEM, VMEM],
        out_specs=(VMEM, VMEM),
        scratch_shapes=[
            pltpu.VMEM((N, N), F32),
            pltpu.VMEM((NB, 2 * NB), F32),
            pltpu.VMEM((NB, NB), F32),
            pltpu.VMEM((6 * NB, N), BF),
            pltpu.VMEM((6 * NB, N), BF),
        ],
        compiler_params=params(40),
        cost_estimate=pl.CostEstimate(flops=10**10, bytes_accessed=4 * 2**20, transcendentals=0),
        name="transform",
    )(scal, ga, gb, drive)


def update_kernel(t_ref, corr_ref, x_ref, keep, send):
    acc = jnp.dot(t_ref[...], x_ref[...], preferred_element_type=F32)
    acc = acc[:NB] + corr_ref[:, 0:1] * acc[NB : NB + 1]
    keep[...] = acc[:64].astype(BF)
    send[...] = acc[64:].astype(BF)


def update(t, corr, x):
    part = jax.ShapeDtypeStruct((64, HALF), BF)
    width = 512
    out = pl.BlockSpec((64, width), lambda i: (0, i))
    return pl.pallas_call(
        update_kernel,
        grid=(HALF // width,),
        out_shape=(part, part),
        in_specs=[
            pl.BlockSpec((NB + 16, N), lambda i: (0, 0)),
            pl.BlockSpec((NB, NB), lambda i: (0, 0)),
            pl.BlockSpec((N, width), lambda i: (0, i)),
        ],
        out_specs=(out, out),
        compiler_params=params(32),
        cost_estimate=pl.CostEstimate(flops=2 * NB * N * HALF, bytes_accessed=5 * 2**20, transcendentals=0),
        name="update",
    )(t, corr, x)


def swap(x):
    return lax.ppermute(x, "core", [(0, 1), (1, 0)])


CHIPS = ("yh", "x")
PLANE = ("yh", "x", "yl")


def gather(x, axes, size):
    return lax.all_to_all(jnp.broadcast_to(x[None], (size, *x.shape)), axes, 0, 0, tiled=True)


def per_device(background_samples, sensor_cell_offsets, sensor_data, sensor_sigma_list):
    core = lax.axis_index("core")
    scal = jnp.stack([lax.axis_index("yh"), lax.axis_index("x"), core]).astype(jnp.int32)
    xa = lax.all_to_all(background_samples.reshape(64, NK, PART), CHIPS, 1, 0)
    xb = swap(xa)
    first = core == 0
    low, high = background_samples[:, :HALF], background_samples[:, HALF:]
    mine = jnp.where(first, low, high)
    got = swap(jnp.where(first, high, low))
    block = jnp.where(first, jnp.concatenate([mine, got]), jnp.concatenate([got, mine]))
    samples = lax.all_gather(block, CHIPS, axis=0, tiled=True)
    ws = obs_sums(scal, sensor_cell_offsets, sensor_data, sensor_sigma_list)
    part = gram_part(scal, ws, xa, xb)
    part = jnp.sum(lax.all_to_all(part, PLANE, 0, 0, tiled=True), axis=0)
    part = jnp.pad(part, ((0, 40), (0, 0))).reshape(8, 24, NB)
    part = jnp.sum(lax.all_to_all(part, ("z",), 0, 0, tiled=True), axis=0)
    part = gather(part, ("z",), 8).reshape(192, NB)
    ga = gather(part[:GROWS], PLANE, 16).reshape(16 * GROWS, NB)
    gb = swap(ga)
    t, corr = transform(scal, ga, gb, part[GROWS : GROWS + 8])
    keep, send = update(t, corr, samples)
    got = swap(send)
    return jnp.where(first, jnp.concatenate([keep, got], axis=1), jnp.concatenate([got, keep], axis=1))


def solution(mesh):
    names = ("yh", "x", "core", "z", "yl")
    split = Mesh(mesh.devices.reshape(2, 4, 2, 8, 2), names)
    mem, sp = names[:3], names[3:]
    return jax.shard_map(
        per_device,
        mesh=split,
        in_specs=(P(mem, sp), P(sp), P(sp), P(sp)),
        out_specs=P(mem, sp),
        check_vma=False,
    )
```

time: 199 us -> 170 us (0.85)
  waiting for transfers between devices: 42.5 us -> 4.82 us
  starting transfers between devices: 37.9 us -> 7.96 us
  blocking collectives: 60.3 us -> 84.6 us
  between operations: 0.09 us -> 13.5 us
  Pallas kernels: 55.8 us -> 53 us
  local copies, waits for them, and re-layouts: 0.13 us -> 2.64 us
    ppermute x7 -> x0, waiting for transfers between devices: 36.1 us -> none  [from_chip(): return lax.ppermute(x, ('yh', 'x'), pairs)]
    all_to_all x1 -> x3, blocking collectives: 21.3 us -> 52.6 us  [the longest x1 22.6 us: per_device(): part = jnp.sum(lax.all_to_all(part, PLANE, 0, 0, tiled=True), axis=0)]
    ppermute x7 -> x0, starting transfers between devices: 29 us -> none  [from_chip(): return lax.ppermute(x, ('yh', 'x'), pairs)]
    all_to_all x2, blocking collectives: 39 us -> 32 us  [gather(): lax.all_to_all(jnp.broadcast_to(x[None], (size, *x.shape)), axes, 0, 0, t...]
    pallas_call x4, Pallas kernels: 55.8 us -> 53 us  [the longest x1 47.3 us: transform(): pl.pallas_call(transform_kernel, out_shape=(jax.ShapeDtypeStruct((NB + 16...]
    unnamed x6 -> x11, local copies, waits for them, and re-layouts: 0.01 us -> 2.38 us
  transfers between devices with their start and end apart: 11 -> 5, of which waited for: 9 -> 3; matrix products, arithmetic and copies ran while one was open for 0% -> 0% of each run, Pallas kernels for 1% -> 30%
where the time goes in v2:
time: 170 us
  blocking collectives  84.6 us (50%)
  Pallas kernels  53 us (31%)
  between operations  13.5 us (8%)
  starting transfers between devices  7.96 us (5%)
  waiting for transfers between devices  4.82 us (3%)
  other arithmetic  3.1 us (2%)
  local copies, waits for them, and re-layouts  2.64 us (2%)
    pallas_call x1, Pallas kernels, transform(): pl.pallas_call(transform_kernel, out_shape=(jax.ShapeDtypeStruct((NB + 16...  47.3 us
    all_to_all x2, blocking collectives, gather(): lax.all_to_all(jnp.broadcast_to(x[None], (size, *x.shape)), axes, 0, 0, t...  32 us
    all_to_all x1, blocking collectives, per_device(): part = jnp.sum(lax.all_to_all(part, PLANE, 0, 0, tiled=True), axis=0)  22.6 us
    all_to_all x1, blocking collectives, per_device(): xa = lax.all_to_all(background_samples.reshape(64, NK, PART), CHIPS, 1, 0)  15.7 us
    all_to_all x1, blocking collectives, per_device(): part = jnp.sum(lax.all_to_all(part, ('z',), 0, 0, tiled=True), axis=0)  14.4 us
    ppermute x4, starting transfers between devices, swap(): return lax.ppermute(x, 'core', [(0, 1), (1, 0)])  7.96 us
    ppermute x4, waiting for transfers between devices, swap(): return lax.ppermute(x, 'core', [(0, 1), (1, 0)])  4.8 us
  transfers between devices with their start and end apart: 5, of which 3 were waited for; matrix products, arithmetic and copies ran while one was open for 0% of the time, Pallas kernels for 30%

profile of v2, /device:TPU:1, one launch (start us, length us, event | category | flops | bytes accessed | tf_op | source)
XLA Modules:
  0.0 169.7 jit_solution(13211023490885165020)
XLA Ops:
  6.5 0.0 all-gather.2.cloned.1.call-start
  6.5 1.1 broadcast_select_fusion.1
  7.7 3.3 %collective-permute-start.2 = (bf16[64,2048]{1,0:T(8,128)(2,1)S(1)}, bf16[64,2048]{1,0:T(8,128)(2,1)S(1)}, u32[]{:S(2)}, u32[]{:S(2)}) collective-permute-start(bf16[64,2048]{1,0:T(8,128)(2,1)S(1)} %get-tuple-element.14), channel_id=1, source_target_pairs={{0,16},{16,0},{1,17},{17,1},{2,18},{18,2},{3,19},{19,3},{4,20},{20... | collective-permute-start | bytes 786440 | tf_op jit(solution)/shard_map/ppermute | solution.py:285
  11.0 1.2 collective-permute-done.2
  12.2 0.9 maximum_select_fusion
  13.1 0.0 all-gather.2.cloned.1.call-update
  13.1 0.2 copy.8
  13.3 0.0 copy-start.1
  13.3 0.0 copy-start.2
  13.3 0.0 copy-start.3
  13.3 0.2 copy.7
  13.5 15.7 %all_to_all.35 = bf16[1,64,8,512]{3,1,0,2:T(8,128)(2,1)S(1)} all-to-all(bf16[1,64,8,512]{3,1,0,2:T(8,128)(2,1)S(1)} %copy.7), channel_id=1, replica_groups=mesh['yh'=2,'x'=4,'core'=2,'z'=8,'yl'=2] {'yh','x'}, dimensions={2} | all-to-all | bytes 1048576 | tf_op jit(solution)/shard_map/all_to_all | solution.py:299
  29.2 1.6 collective-permute-start
  30.7 0.1 pad_add_fusion.scal
  30.8 1.8 %obs_sums.1.ws_ref = f32[8,512]{1,0:T(8,128)S(1)} custom-call(s32[3]{0:T(128)S(1)} %pad_add_fusion.scal, s32[64,128]{1,0:T(8,128)S(1)} %bitcast.22, f32[64,128]{1,0:T(8,128)S(1)} %bitcast.23, f32[64,128]{1,0:T(8,128)S(1)} %bitcast.24), custom_call_target="tpu_custom_call" | custom-call | flops 67108864 | bytes 200000 | tf_op jit(solution)/shard_map/obs_sums/pallas_call | solution.py:71
  32.6 0.0 collective-permute-done.xb
  32.6 2.1 %gram_part.1 = f32[16,152,128]{2,1,0:T(8,128)S(1)} custom-call(s32[3]{0:T(128)S(1)} %pad_add_fusion.scal, f32[8,512]{1,0:T(8,128)S(1)} %obs_sums.1.ws_ref, bf16[8,64,512]{2,1,0:T(8,128)(2,1)S(1)} %bitcast.19, bf16[8,64,512]{2,1,0:T(8,128)(2,1)S(1)} %collective-permute-done.xb), custom_call_target="tpu_custom_call" | custom-call | flops 301989888 | bytes 3145728 | tf_op jit(solution)/shard_map/gram_part/pallas_call | solution.py:117
  34.7 22.6 %all_to_all.36 = f32[16,152,128]{2,1,0:T(8,128)S(1)} all-to-all(f32[16,152,128]{2,1,0:T(8,128)S(1)} %gram_part.1), channel_id=1, replica_groups=mesh['yh'=2,'x'=4,'core'=2,'z'=8,'yl'=2] {'yh','x','yl'}, dimensions={0} | all-to-all | bytes 2490368 | tf_op jit(solution)/shard_map/all_to_all | solution.py:309
  57.3 0.1 reduce_sum.18
  57.4 14.4 %all_to_all.37 = f32[8,24,128]{2,1,0:T(8,128)S(1)} all-to-all(f32[8,24,128]{2,1,0:T(8,128)S(1)} %bitcast.27), channel_id=1, replica_groups=mesh['yh'=2,'x'=4,'core'=2,'z'=8,'yl'=2] {'z'}, dimensions={0} | all-to-all | bytes 196608 | tf_op jit(solution)/shard_map/all_to_all | solution.py:311
  71.8 10.0 %all_to_all.38 = f32[8,24,128]{2,1,0:T(8,128)S(1)} all-to-all(f32[8,24,128]{2,1,0:T(8,128)S(1)} %broadcast_in_dim.6), channel_id=1, replica_groups=mesh['yh'=2,'x'=4,'core'=2,'z'=8,'yl'=2] {'z'}, dimensions={0} | all-to-all | bytes 196608 | tf_op jit(solution)/shard_map/all_to_all | solution.py:293
  81.7 0.1 broadcast_in_dim.16
  81.8 22.1 %all_to_all.39 = f32[16,144,128]{2,1,0:T(8,128)S(1)} all-to-all(f32[16,144,128]{2,1,0:T(8,128)S(1)} %broadcast_in_dim.16), channel_id=1, replica_groups=mesh['yh'=2,'x'=4,'core'=2,'z'=8,'yl'=2] {'yh','x','yl'}, dimensions={0} | all-to-all | bytes 2359296 | tf_op jit(solution)/shard_map/all_to_all | solution.py:293
  103.9 2.6 %collective-permute-start.1 = (f32[2304,128]{1,0:T(8,128)S(1)}, f32[2304,128]{1,0:T(8,128)S(1)}, u32[]{:S(2)}, u32[]{:S(2)}) collective-permute-start(f32[2304,128]{1,0:T(8,128)S(1)} %bitcast.20), channel_id=1, source_target_pairs={{0,16},{16,0},{1,17},{17,1},{2,18},{18,2},{3,19},{19,3},{4,20},{20... | collective-permute-start | bytes 3538952 | tf_op jit(solution)/shard_map/ppermute | solution.py:285
  106.4 2.5 %collective-permute-done.1.gb = f32[2304,128]{1,0:T(8,128)S(1)} collective-permute-done((f32[2304,128]{1,0:T(8,128)S(1)}, f32[2304,128]{1,0:T(8,128)S(1)}, u32[]{:S(2)}, u32[]{:S(2)}) %collective-permute-start.1) | collective-permute-done | bytes 1179680 | tf_op jit(solution)/shard_map/ppermute | solution.py:285
  108.9 47.3 %transform.1 = (bf16[144,1024]{1,0:T(8,128)(2,1)S(1)}, f32[128,128]{1,0:T(8,128)S(1)}) custom-call(s32[3]{0:T(128)S(1)} %pad_add_fusion.scal, f32[2304,128]{1,0:T(8,128)S(1)} %bitcast.21, f32[2304,128]{1,0:T(8,128)S(1)} %collective-permute-done.1.gb, f32[8,128]{1,0:T(8,128)S(1)} %slice.18.drive_ref), custom_call_target="tpu_custom_call" | custom-call | flops 10000000000 | bytes 4194304 | tf_op jit(solution)/shard_map/transform/pallas_call | solution.py:239
  156.2 0.0 all-gather.2.cloned.1.call-done.x_ref
  156.2 2.2 %copy-done = bf16[1024,2048]{1,0:T(8,128)(2,1)S(1)} copy-done((bf16[1024,2048]{1,0:T(8,128)(2,1)S(1)}, bf16[1024,2048]{1,0:T(8,128)(2,1)}, u32[]{:S(2)}) %copy-start) | copy-done | bytes 4194328
  158.4 1.8 %update.1 = (bf16[64,2048]{1,0:T(8,128)(2,1)S(1)}, bf16[64,2048]{1,0:T(8,128)(2,1)S(1)}) custom-call(bf16[144,1024]{1,0:T(8,128)(2,1)S(1)} %get-tuple-element.9.t_ref, f32[128,128]{1,0:T(8,128)S(1)} %get-tuple-element.10.corr_ref, bf16[1024,2048]{1,0:T(8,128)(2,1)S(1)} %copy-done), custom_call_target="tpu_custom_call" | custom-call | flops 536870912 | bytes 5242880 | tf_op jit(solution)/shard_map/update/pallas_call | solution.py:268
  160.3 0.5 collective-permute-start.3
  160.7 1.2 collective-permute-done.3
  161.9 0.9 maximum_select_fusion.1
  (11 shorter events, 0.0 us)
Async XLA Ops:
  6.5 149.7 %all-gather.2.cloned.1.call-start = ((), (), s32[]{:S(2)}) async-start(), calls=%async_computation.5 | async-start | bytes 4718592 | tf_op jit(solution)/shard_map/all_gather | solution.py:306
  6.5 6.5 %copy-start.4 = (bf16[64,4096]{1,0:T(8,128)(2,1)S(1)}, bf16[64,4096]{1,0:T(8,128)(2,1)}, u32[]{:S(2)}) copy-start(bf16[64,4096]{1,0:T(8,128)(2,1)} %param.4) | copy-start | bytes 1572868
  7.7 4.5 %collective-permute-start.2 = (bf16[64,2048]{1,0:T(8,128)(2,1)S(1)}, bf16[64,2048]{1,0:T(8,128)(2,1)S(1)}, u32[]{:S(2)}, u32[]{:S(2)}) collective-permute-start(bf16[64,2048]{1,0:T(8,128)(2,1)S(1)} %get-tuple-element.14), channel_id=1, source_target_pairs={{0,16},{16,0},{1,17},{17,1},{2,18},{18,2},{3,19},{19,3},{4,20},{20... | collective-permute-start | bytes 786440 | tf_op jit(solution)/shard_map/ppermute | solution.py:285
  13.3 17.5 %copy-start.1 = (s32[8192]{0:T(1024)S(1)}, s32[8192]{0:T(1024)}, u32[]{:S(2)}) copy-start(s32[8192]{0:T(1024)} %param.5) | copy-start | bytes 98308
  13.3 17.5 %copy-start.2 = (f32[8192]{0:T(1024)S(1)}, f32[8192]{0:T(1024)}, u32[]{:S(2)}) copy-start(f32[8192]{0:T(1024)} %param.6) | copy-start | bytes 98308
  13.3 17.5 %copy-start.3 = (f32[8192]{0:T(1024)S(1)}, f32[8192]{0:T(1024)}, u32[]{:S(2)}) copy-start(f32[8192]{0:T(1024)} %param.7) | copy-start | bytes 98308
  29.2 3.5 %collective-permute-start = (bf16[8,64,512]{2,1,0:T(8,128)(2,1)S(1)}, bf16[8,64,512]{2,1,0:T(8,128)(2,1)S(1)}, u32[]{:S(2)}, u32[]{:S(2)}) collective-permute-start(bf16[8,64,512]{2,1,0:T(8,128)(2,1)S(1)} %bitcast.18), channel_id=1, source_target_pairs={{0,16},{16,0},{1,17},{17,1},{2,18},{18,2},{3,19},{19,3},{4,20},{20... | collective-permute-start | bytes 1572872 | tf_op jit(solution)/shard_map/ppermute | solution.py:285
  103.9 5.1 %collective-permute-start.1 = (f32[2304,128]{1,0:T(8,128)S(1)}, f32[2304,128]{1,0:T(8,128)S(1)}, u32[]{:S(2)}, u32[]{:S(2)}) collective-permute-start(f32[2304,128]{1,0:T(8,128)S(1)} %bitcast.20), channel_id=1, source_target_pairs={{0,16},{16,0},{1,17},{17,1},{2,18},{18,2},{3,19},{19,3},{4,20},{20... | collective-permute-start | bytes 3538952 | tf_op jit(solution)/shard_map/ppermute | solution.py:285
  156.2 2.2 %copy-start = (bf16[1024,2048]{1,0:T(8,128)(2,1)S(1)}, bf16[1024,2048]{1,0:T(8,128)(2,1)}, u32[]{:S(2)}) copy-start(bf16[1024,2048]{1,0:T(8,128)(2,1)} %all-gather.2.cloned.1.call-done.x_ref) | copy-start | bytes 12582916
  160.3 1.6 collective-permute-start.3
Sparse Core Ops, SparseCore 0:
  13.2 82.2 all-gather.1

commit v3 on v2

--- a/solution.py
+++ b/solution.py
@@ -12,7 +12,6 @@
 N = 1024
 CELLS = 4096
 OBS = 8192
-HALF = CELLS // 2
 NB = 128
 SB = 8
 NK = N // NB
@@ -84,12 +83,13 @@
     return [(4 * core + i, d) for d in range(4) for i in range(4)] + [(2 * core + i, 4) for i in range(2)]
 
 
-def gram_kernel(scal, ws_ref, xa, xb, out_ref, b):
+def gram_kernel(scal, ws_ref, xa, xb, out_ref, mean_ref, b):
     core = scal[2]
     total = jnp.zeros((1, PART), F32)
     for i in range(NK):
         total = total + jnp.sum(xa[i].astype(F32), axis=0, keepdims=True) + jnp.sum(xb[i].astype(F32), axis=0, keepdims=True)
     mean = total * (1.0 / N)
+    mean_ref[...] = jnp.broadcast_to(mean, (8, PART))
     w = ws_ref[0:1, :]
     root = jnp.sqrt(w)
     for i in range(NK):
@@ -116,9 +116,9 @@
 def gram_part(scal, ws, xa, xb):
     return pl.pallas_call(
         gram_kernel,
-        out_shape=jax.ShapeDtypeStruct((16, GROWS + 8, NB), F32),
+        out_shape=(jax.ShapeDtypeStruct((16, GROWS + 8, NB), F32), jax.ShapeDtypeStruct((8, PART), F32)),
         in_specs=[SMEM] + [VMEM] * 3,
-        out_specs=VMEM,
+        out_specs=(VMEM, VMEM),
         scratch_shapes=[pltpu.VMEM((N, PART), BF)],
         compiler_params=params(32),
         cost_estimate=pl.CostEstimate(flops=2 * NB * NB * 18 * PART, bytes_accessed=3 * 2**20, transcendentals=0),
@@ -199,9 +199,8 @@
     lax.fori_loop(0, NK, step, 0)
 
 
-def transform_kernel(scal, ga, gb, drive_ref, t_ref, corr_ref, z, dz, vb, lhs, rhs):
+def transform_kernel(scal, ga, gb, drive_ref, xa, xb, mean_ref, out_ref, z, dz, vb, lhs, rhs, t, x):
     core = scal[2]
-    me = scal[0] * 4 + scal[1]
     rows = lax.broadcasted_iota(jnp.int32, (NB, NB), 0)
     ridge = jnp.where(rows == lax.broadcasted_iota(jnp.int32, (NB, NB), 1), N - 1.0, 0.0)
     zero_core = (rows * 0 + core) == 0
@@ -228,57 +227,38 @@
         return acc
 
     weights = jnp.sum(lax.fori_loop(0, N // 64, weigh, jnp.zeros((8, N), F32)), axis=0, keepdims=True)
-    own = jnp.concatenate([z[at(2 * me + core, 64), :], z[at(2 * me + 1 - core, 64), :]], axis=0)
-    t = (own * math.sqrt(N - 1) + weights).astype(BF)
-    t_ref[0:NB, :] = t
-    t_ref[NB:, :] = jnp.full((16, N), 1.0 / N, BF)
-    corr_ref[...] = jnp.broadcast_to(1.0 - jnp.sum(t.astype(F32), axis=1, keepdims=True), corr_ref.shape)
-
-
-def transform(scal, ga, gb, drive):
+    corr = []
+    for i in range(NK):
+        own = (z[at(2 * i + core, 64), :] * math.sqrt(N - 1) + weights).astype(BF)
+        t[i * 64 : (i + 1) * 64, :] = own
+        corr.append(1.0 - jnp.sum(own.astype(F32), axis=1, keepdims=True))
+        x[at(2 * i + core, 64), :] = xa[i]
+        x[at(2 * i + 1 - core, 64), :] = xb[i]
+    for i in range(0, NK, 2):
+        y = jnp.dot(t[i * 64 : (i + 2) * 64, :], x[...], preferred_element_type=F32)
+        for j in range(2):
+            out_ref[i + j] = (y[64 * j : 64 * j + 64] + corr[i + j] * mean_ref[0:1, :]).astype(BF)
+
+
+def transform(scal, ga, gb, drive, xa, xb, mean):
     return pl.pallas_call(
         transform_kernel,
-        out_shape=(jax.ShapeDtypeStruct((NB + 16, N), BF), jax.ShapeDtypeStruct((NB, NB), F32)),
-        in_specs=[SMEM, VMEM, VMEM, VMEM],
-        out_specs=(VMEM, VMEM),
+        out_shape=jax.ShapeDtypeStruct((NK, 64, PART), BF),
+        in_specs=[SMEM] + [VMEM] * 6,
+        out_specs=VMEM,
         scratch_shapes=[
             pltpu.VMEM((N, N), F32),
             pltpu.VMEM((NB, 2 * NB), F32),
             pltpu.VMEM((NB, NB), F32),
             pltpu.VMEM((6 * NB, N), BF),
             pltpu.VMEM((6 * NB, N), BF),
+            pltpu.VMEM((N // 2, N), BF),
+            pltpu.VMEM((N, PART), BF),
         ],
         compiler_params=params(40),
         cost_estimate=pl.CostEstimate(flops=10**10, bytes_accessed=4 * 2**20, transcendentals=0),
         name="transform",
-    )(scal, ga, gb, drive)
-
-
-def update_kernel(t_ref, corr_ref, x_ref, keep, send):
-    acc = jnp.dot(t_ref[...], x_ref[...], preferred_element_type=F32)
-    acc = acc[:NB] + corr_ref[:, 0:1] * acc[NB : NB + 1]
-    keep[...] = acc[:64].astype(BF)
-    send[...] = acc[64:].astype(BF)
-
-
-def update(t, corr, x):
-    part = jax.ShapeDtypeStruct((64, HALF), BF)
-    width = 512
-    out = pl.BlockSpec((64, width), lambda i: (0, i))
-    return pl.pallas_call(
-        update_kernel,
-        grid=(HALF // width,),
-        out_shape=(part, part),
-        in_specs=[
-            pl.BlockSpec((NB + 16, N), lambda i: (0, 0)),
-            pl.BlockSpec((NB, NB), lambda i: (0, 0)),
-            pl.BlockSpec((N, width), lambda i: (0, i)),
-        ],
-        out_specs=(out, out),
-        compiler_params=params(32),
-        cost_estimate=pl.CostEstimate(flops=2 * NB * N * HALF, bytes_accessed=5 * 2**20, transcendentals=0),
-        name="update",
-    )(t, corr, x)
+    )(scal, ga, gb, drive, xa, xb, mean)
 
 
 def swap(x):
@@ -298,24 +278,16 @@
     scal = jnp.stack([lax.axis_index("yh"), lax.axis_index("x"), core]).astype(jnp.int32)
     xa = lax.all_to_all(background_samples.reshape(64, NK, PART), CHIPS, 1, 0)
     xb = swap(xa)
-    first = core == 0
-    low, high = background_samples[:, :HALF], background_samples[:, HALF:]
-    mine = jnp.where(first, low, high)
-    got = swap(jnp.where(first, high, low))
-    block = jnp.where(first, jnp.concatenate([mine, got]), jnp.concatenate([got, mine]))
-    samples = lax.all_gather(block, CHIPS, axis=0, tiled=True)
     ws = obs_sums(scal, sensor_cell_offsets, sensor_data, sensor_sigma_list)
-    part = gram_part(scal, ws, xa, xb)
+    part, mean = gram_part(scal, ws, xa, xb)
     part = jnp.sum(lax.all_to_all(part, PLANE, 0, 0, tiled=True), axis=0)
     part = jnp.pad(part, ((0, 40), (0, 0))).reshape(8, 24, NB)
     part = jnp.sum(lax.all_to_all(part, ("z",), 0, 0, tiled=True), axis=0)
     part = gather(part, ("z",), 8).reshape(192, NB)
     ga = gather(part[:GROWS], PLANE, 16).reshape(16 * GROWS, NB)
     gb = swap(ga)
-    t, corr = transform(scal, ga, gb, part[GROWS : GROWS + 8])
-    keep, send = update(t, corr, samples)
-    got = swap(send)
-    return jnp.where(first, jnp.concatenate([keep, got], axis=1), jnp.concatenate([got, keep], axis=1))
+    out = transform(scal, ga, gb, part[GROWS : GROWS + 8], xa, xb, mean)
+    return lax.all_to_all(out, CHIPS, 0, 1).reshape(64, CELLS)
 
 
 def solution(mesh):

time: 170 us -> 161 us (0.947)
  between operations: 13.5 us -> 0.1 us
  blocking collectives: 84.6 us -> 96.6 us
  other arithmetic: 3.1 us -> 0.15 us
  waiting for transfers between devices: 4.82 us -> 2.47 us
    all_to_all x0 -> x1, blocking collectives: none -> 14.4 us  [per_device(): return lax.all_to_all(out, CHIPS, 0, 1).reshape(64, CELLS)]
    all_to_all x2, blocking collectives: 32 us -> 27.3 us  [gather(): lax.all_to_all(jnp.broadcast_to(x[None], (size, *x.shape)), axes, 0, 0, t...]
    select_n x3 -> x0, other arithmetic: 2.94 us -> none  [the longest x1 1.13 us: per_device(): mine = jnp.where(first, low, high)]
    ppermute x4 -> x2, waiting for transfers between devices: 4.8 us -> 2.47 us  [swap(): return lax.ppermute(x, 'core', [(0, 1), (1, 0)])]
    all_to_all x1, blocking collectives: 15.7 us -> 18 us  [per_device(): xa = lax.all_to_all(background_samples.reshape(64, NK, PART), CHIPS, 1, 0)]
    pallas_call x3 -> x2, Pallas kernels: 51.2 us -> 49.9 us  [the longest x1 47.9 us: transform(): pl.pallas_call(transform_kernel, out_shape=jax.ShapeDtypeStruct((NK, 64,...]
    ppermute x4 -> x2, starting transfers between devices: 7.96 us -> 7.1 us  [swap(): return lax.ppermute(x, 'core', [(0, 1), (1, 0)])]
  transfers between devices with their start and end apart: 5 -> 2, of which waited for: 3 -> 1; matrix products, arithmetic and copies ran while one was open for 0% -> 0% of each run, Pallas kernels for 30% -> 1%
where the time goes in v3:
time: 161 us; the launch traced here: 160 us
  blocking collectives  96.6 us (60%)
  Pallas kernels  51.7 us (32%)
  starting transfers between devices  7.1 us (4%)
  waiting for transfers between devices  2.47 us (2%)
  local copies, waits for them, and re-layouts  2.33 us (1%)
    pallas_call x1, Pallas kernels, transform(): pl.pallas_call(transform_kernel, out_shape=jax.ShapeDtypeStruct((NK, 64,...  47.9 us
    all_to_all x2, blocking collectives, gather(): lax.all_to_all(jnp.broadcast_to(x[None], (size, *x.shape)), axes, 0, 0, t...  27.3 us
    all_to_all x1, blocking collectives, per_device(): part = jnp.sum(lax.all_to_all(part, PLANE, 0, 0, tiled=True), axis=0)  21.3 us
    all_to_all x1, blocking collectives, per_device(): xa = lax.all_to_all(background_samples.reshape(64, NK, PART), CHIPS, 1, 0)  18 us
    all_to_all x1, blocking collectives, per_device(): part = jnp.sum(lax.all_to_all(part, ('z',), 0, 0, tiled=True), axis=0)  15.6 us
    all_to_all x1, blocking collectives, per_device(): return lax.all_to_all(out, CHIPS, 0, 1).reshape(64, CELLS)  14.4 us
    ppermute x2, starting transfers between devices, swap(): return lax.ppermute(x, 'core', [(0, 1), (1, 0)])  7.1 us
  transfers between devices with their start and end apart: 2, of which 1 were waited for; matrix products, arithmetic and copies ran while one was open for 0% of the time, Pallas kernels for 1%

profile of v3, /device:TPU:1, one launch (start us, length us, event | category | flops | bytes accessed | tf_op | source)
XLA Modules:
  0.0 160.5 jit_solution(1920189810271117488)
XLA Ops:
  0.0 1.2 copy.13
  1.2 0.0 copy-start
  1.2 0.0 copy-start.1
  1.2 0.0 copy-start.2
  1.3 0.2 copy.10
  1.4 18.0 %all_to_all.50 = bf16[1,64,8,512]{3,1,0,2:T(8,128)(2,1)S(1)} all-to-all(bf16[1,64,8,512]{3,1,0,2:T(8,128)(2,1)S(1)} %copy.10), channel_id=1, replica_groups=mesh['yh'=2,'x'=4,'core'=2,'z'=8,'yl'=2] {'yh','x'}, dimensions={2} | all-to-all | bytes 1048576 | tf_op jit(solution)/shard_map/all_to_all | solution.py:279
  19.4 1.9 %collective-permute-start = (bf16[8,64,512]{2,1,0:T(8,128)(2,1)S(1)}, bf16[8,64,512]{2,1,0:T(8,128)(2,1)S(1)}, u32[]{:S(2)}, u32[]{:S(2)}) collective-permute-start(bf16[8,64,512]{2,1,0:T(8,128)(2,1)S(1)} %bitcast.32), channel_id=1, source_target_pairs={{0,16},{16,0},{1,17},{17,1},{2,18},{18,2},{3,19},{19,3},{4,20},{20... | collective-permute-start | bytes 1572872 | tf_op jit(solution)/shard_map/ppermute | solution.py:265
  21.2 0.1 pad_add_fusion.scal
  21.3 0.0 copy-done
  21.3 0.0 copy-done.1
  21.3 0.0 copy-done.2
  21.3 1.8 %obs_sums.1.ws_ref = f32[8,512]{1,0:T(8,128)S(1)} custom-call(s32[3]{0:T(128)S(1)} %pad_add_fusion.scal, s32[64,128]{1,0:T(8,128)S(1)} %bitcast.36, f32[64,128]{1,0:T(8,128)S(1)} %bitcast.37, f32[64,128]{1,0:T(8,128)S(1)} %bitcast.38), custom_call_target="tpu_custom_call" | custom-call | flops 67108864 | bytes 200000 | tf_op jit(solution)/shard_map/obs_sums/pallas_call | solution.py:70
  23.1 0.0 collective-permute-done.xb
  23.1 2.0 %gram_part.1 = (f32[16,152,128]{2,1,0:T(8,128)S(1)}, f32[8,512]{1,0:T(8,128)S(1)}) custom-call(s32[3]{0:T(128)S(1)} %pad_add_fusion.scal, f32[8,512]{1,0:T(8,128)S(1)} %obs_sums.1.ws_ref, bf16[8,64,512]{2,1,0:T(8,128)(2,1)S(1)} %bitcast.33, bf16[8,64,512]{2,1,0:T(8,128)(2,1)S(1)} %collective-permute-done.xb), custom_call_target="tpu_custom_call" | custom-call | flops 301989888 | bytes 3145728 | tf_op jit(solution)/shard_map/gram_part/pallas_call | solution.py:117
  25.2 21.3 %all_to_all.51 = f32[16,152,128]{2,1,0:T(8,128)S(1)} all-to-all(f32[16,152,128]{2,1,0:T(8,128)S(1)} %get-tuple-element.7), channel_id=1, replica_groups=mesh['yh'=2,'x'=4,'core'=2,'z'=8,'yl'=2] {'yh','x','yl'}, dimensions={0} | all-to-all | bytes 2490368 | tf_op jit(solution)/shard_map/all_to_all | solution.py:283
  46.5 0.1 reduce_sum.18
  46.6 15.6 %all_to_all.52 = f32[8,24,128]{2,1,0:T(8,128)S(1)} all-to-all(f32[8,24,128]{2,1,0:T(8,128)S(1)} %bitcast.42), channel_id=1, replica_groups=mesh['yh'=2,'x'=4,'core'=2,'z'=8,'yl'=2] {'z'}, dimensions={0} | all-to-all | bytes 196608 | tf_op jit(solution)/shard_map/all_to_all | solution.py:285
  62.2 10.0 %all_to_all.53 = f32[8,24,128]{2,1,0:T(8,128)S(1)} all-to-all(f32[8,24,128]{2,1,0:T(8,128)S(1)} %broadcast_in_dim.8), channel_id=1, replica_groups=mesh['yh'=2,'x'=4,'core'=2,'z'=8,'yl'=2] {'z'}, dimensions={0} | all-to-all | bytes 196608 | tf_op jit(solution)/shard_map/all_to_all | solution.py:273
  72.1 0.1 broadcast_in_dim.19
  72.2 17.4 %all_to_all.54 = f32[16,144,128]{2,1,0:T(8,128)S(1)} all-to-all(f32[16,144,128]{2,1,0:T(8,128)S(1)} %broadcast_in_dim.19), channel_id=1, replica_groups=mesh['yh'=2,'x'=4,'core'=2,'z'=8,'yl'=2] {'yh','x','yl'}, dimensions={0} | all-to-all | bytes 2359296 | tf_op jit(solution)/shard_map/all_to_all | solution.py:273
  89.6 5.2 %collective-permute-start.1 = (f32[2304,128]{1,0:T(8,128)S(1)}, f32[2304,128]{1,0:T(8,128)S(1)}, u32[]{:S(2)}, u32[]{:S(2)}) collective-permute-start(f32[2304,128]{1,0:T(8,128)S(1)} %bitcast.30), channel_id=1, source_target_pairs={{0,16},{16,0},{1,17},{17,1},{2,18},{18,2},{3,19},{19,3},{4,20},{20... | collective-permute-start | bytes 3538952 | tf_op jit(solution)/shard_map/ppermute | solution.py:265
  94.8 2.5 %collective-permute-done.1.gb = f32[2304,128]{1,0:T(8,128)S(1)} collective-permute-done((f32[2304,128]{1,0:T(8,128)S(1)}, f32[2304,128]{1,0:T(8,128)S(1)}, u32[]{:S(2)}, u32[]{:S(2)}) %collective-permute-start.1) | collective-permute-done | bytes 1179680 | tf_op jit(solution)/shard_map/ppermute | solution.py:265
  97.3 47.9 %transform.1 = bf16[8,64,512]{2,1,0:T(8,128)(2,1)S(1)} custom-call(s32[3]{0:T(128)S(1)} %pad_add_fusion.scal, f32[2304,128]{1,0:T(8,128)S(1)} %bitcast.31, f32[2304,128]{1,0:T(8,128)S(1)} %collective-permute-done.1.gb, f32[8,128]{1,0:T(8,128)S(1)} %slice.10.drive_ref, bf16[8,64,512]{2,1,0:T(8,128)(2,1)S(1)} %bitcast.34, ...), custom_call_target="tpu_custom_call" | custom-call | flops 10000000000 | bytes 4194304 | tf_op jit(solution)/shard_map/transform/pallas_call | solution.py:244
  145.2 14.4 %all_to_all.55 = bf16[8,64,1,512]{3,1,2,0:T(8,128)(2,1)S(1)} all-to-all(bf16[8,64,1,512]{3,1,2,0:T(8,128)(2,1)S(1)} %bitcast.35), channel_id=1, replica_groups=mesh['yh'=2,'x'=4,'core'=2,'z'=8,'yl'=2] {'yh','x'}, dimensions={0} | all-to-all | bytes 1048576 | tf_op jit(solution)/shard_map/all_to_all | solution.py:290
  159.6 0.8 copy.14
  (5 shorter events, 0.0 us)
Async XLA Ops:
  1.2 20.1 %copy-start = (s32[8192]{0:T(1024)S(1)}, s32[8192]{0:T(1024)}, u32[]{:S(2)}) copy-start(s32[8192]{0:T(1024)} %param.5) | copy-start | bytes 98308
  1.2 20.1 %copy-start.1 = (f32[8192]{0:T(1024)S(1)}, f32[8192]{0:T(1024)}, u32[]{:S(2)}) copy-start(f32[8192]{0:T(1024)} %param.6) | copy-start | bytes 98308
  1.2 20.1 %copy-start.2 = (f32[8192]{0:T(1024)S(1)}, f32[8192]{0:T(1024)}, u32[]{:S(2)}) copy-start(f32[8192]{0:T(1024)} %param.7) | copy-start | bytes 98308
  19.4 3.8 %collective-permute-start = (bf16[8,64,512]{2,1,0:T(8,128)(2,1)S(1)}, bf16[8,64,512]{2,1,0:T(8,128)(2,1)S(1)}, u32[]{:S(2)}, u32[]{:S(2)}) collective-permute-start(bf16[8,64,512]{2,1,0:T(8,128)(2,1)S(1)} %bitcast.32), channel_id=1, source_target_pairs={{0,16},{16,0},{1,17},{17,1},{2,18},{18,2},{3,19},{19,3},{4,20},{20... | collective-permute-start | bytes 1572872 | tf_op jit(solution)/shard_map/ppermute | solution.py:265
  89.6 7.7 %collective-permute-start.1 = (f32[2304,128]{1,0:T(8,128)S(1)}, f32[2304,128]{1,0:T(8,128)S(1)}, u32[]{:S(2)}, u32[]{:S(2)}) collective-permute-start(f32[2304,128]{1,0:T(8,128)S(1)} %bitcast.30), channel_id=1, source_target_pairs={{0,16},{16,0},{1,17},{17,1},{2,18},{18,2},{3,19},{19,3},{4,20},{20... | collective-permute-start | bytes 3538952 | tf_op jit(solution)/shard_map/ppermute | solution.py:265

commit v4 on v3

--- a/solution.py
+++ b/solution.py
@@ -21,7 +21,6 @@
 VMEM = pl.BlockSpec(memory_space=pltpu.VMEM)
 SMEM = pl.BlockSpec(memory_space=pltpu.SMEM)
 NTDOT = (((1,), (1,)), ((), ()))
-TNDOT = (((0,), (0,)), ((), ()))
 
 
 def params(mib):
@@ -126,77 +125,125 @@
     )(scal, ws, xa, xb)
 
 
-def diag_inverse(dz, vout):
-    for j in range(NB // SB):
+def diag_inverse(dz, vout, thunks):
+    steps = NB // SB
+    done = 0
+    for j in range(steps):
         r0 = j * SB
         rs = [jnp.broadcast_to(dz[r0 + p : r0 + p + 1, 0:NB], (SB, NB)) for p in range(SB)]
         rw = [jnp.broadcast_to(dz[r0 + p : r0 + p + 1, NB : 2 * NB], (SB, NB)) for p in range(SB)]
         e = [[jnp.broadcast_to(rs[q][:, r0 + p : r0 + p + 1], (SB, NB)) for p in range(q + 1)] for q in range(SB)]
-        groups = range(j + 1, NB // SB)
         c = {}
-        for g in groups:
-            blk = dz[g * SB : (g + 1) * SB, 0:NB]
-            c[g] = [jnp.broadcast_to(blk[:, r0 + p : r0 + p + 1], (SB, NB)) for p in range(SB)]
-        for p in range(SB):
-            r = lax.rsqrt(e[p][p])
-            rs[p] = rs[p] * r
-            rw[p] = rw[p] * r
-            f = {q: e[q][p] * r for q in range(p + 1, SB)}
-            for q in range(p + 1, SB):
-                for s in range(p + 1, q + 1):
-                    e[q][s] = e[q][s] - f[q] * f[s]
-            for q in range(p + 1, SB):
-                rs[q] = rs[q] - f[q] * rs[p]
-                rw[q] = rw[q] - f[q] * rw[p]
-            for g in groups:
-                c[g][p] = c[g][p] * r
-                for q in range(p + 1, SB):
-                    c[g][q] = c[g][q] - f[q] * c[g][p]
-        for p in range(SB):
-            vout[r0 + p : r0 + p + 1, :] = rw[p][0:1, :]
-        for g in groups:
+        for g in range(j + 1, steps):
+            below = dz[g * SB : (g + 1) * SB, 0:NB]
+            c[g] = [jnp.broadcast_to(below[:, r0 + p : r0 + p + 1], (SB, NB)) for p in range(SB)]
+
+        def subtract(g, s, w):
             ds = dz[g * SB : (g + 1) * SB, 0:NB]
             dw = dz[g * SB : (g + 1) * SB, NB : 2 * NB]
             for p in range(SB):
-                ds = ds - c[g][p] * rs[p]
-                dw = dw - c[g][p] * rw[p]
+                ds = ds - c[g][p] * s[p]
+                dw = dw - c[g][p] * w[p]
             dz[g * SB : (g + 1) * SB, 0:NB] = ds
             dz[g * SB : (g + 1) * SB, NB : 2 * NB] = dw
+
+        following = range(j + 1, min(j + 2, steps))
+        f, r = [], []
+        for p in range(SB):
+            r.append(lax.rsqrt(e[p][p]))
+            rs[p] = rs[p] * r[p]
+            rw[p] = rw[p] * r[p]
+            f.append({q: e[q][p] * r[p] for q in range(p + 1, SB)})
+            for q in range(p + 1, SB):
+                for s in range(p + 1, q + 1):
+                    e[q][s] = e[q][s] - f[p][q] * f[p][s]
+            for q in range(p + 1, SB):
+                rs[q] = rs[q] - f[p][q] * rs[p]
+                rw[q] = rw[q] - f[p][q] * rw[p]
+            for g in following:
+                c[g][p] = c[g][p] * r[p]
+                for q in range(p + 1, SB):
+                    c[g][q] = c[g][q] - f[p][q] * c[g][p]
+        for p in range(SB):
+            vout[r0 + p : r0 + p + 1, :] = rw[p][0:1, :]
+        for g in following:
+            subtract(g, rs, rw)
+        if j + 2 < steps:
+            for v in (rs, rw):
+                for p in range(SB - 1, -1, -1):
+                    for q in range(p + 1, SB):
+                        v[p] = v[p] - f[p][q] * v[q]
+                    v[p] = v[p] * r[p]
+            for g in range(j + 2, steps):
+                subtract(g, rs, rw)
+        while done < len(thunks) * (j + 1) // steps:
+            thunks[done]()
+            done += 1
+
+
+def blk(i, n=1):
+    return slice(i * NB, (i + n) * NB)
 
 
 def inverse_factor(z, dz, vb, lhs, rhs):
     rows = lax.broadcasted_iota(jnp.int32, (NB, NB), 0)
     eye = jnp.where(rows == lax.broadcasted_iota(jnp.int32, (NB, NB), 1), 1.0, 0.0)
-    zero = jnp.zeros((NB, NB), F32)
-
-    def step(k, carry):
-        ks = at(k, NB)
-        dz[:, 0:NB] = z[ks, ks]
+    pending = []
+    for k in range(NK):
+        dz[:, 0:NB] = z[blk(k), blk(k)]
         dz[:, NB : 2 * NB] = eye
-        diag_inverse(dz, vb)
+        diag_inverse(dz, vb, pending)
+        pending = []
         v = vb[...]
+        side = k % 2
         vh, vm, vl = split3(v)
-        zh, zm, zl = split3(z[ks, :])
         a = jnp.concatenate([vh, vh, vm, vh, vl, vm], axis=1)
-        b = jnp.concatenate([zh, zm, zh, zl, zh, zm], axis=0)
-        z[ks, :] = jnp.dot(a, b, preferred_element_type=F32)
-        z[ks, ks] = v
-        rh, rm, rl = split3(z[ks, :])
-        for i, x in enumerate([rh, rm, rh, rl, rh, rm]):
-            rhs[i * NB : (i + 1) * NB, :] = x
-        for i, x in enumerate([rh, rh, rm, rh, rl, rm]):
-            lhs[i * NB : (i + 1) * NB, :] = x
-
-        def trail(i, carry):
-            si = at(i, NB)
-            z[si, ks] = zero
-            z[si, :] = z[si, :] - lax.dot_general(lhs[:, si], rhs[...], TNDOT, preferred_element_type=F32)
-            z[ks, si] = zero
-            return carry
-
-        return lax.fori_loop(k + 1, NK, trail, carry)
-
-    lax.fori_loop(0, NK, step, 0)
+
+        def put(j, n, r):
+            h, m, l = split3(r)
+            for i, x in enumerate([h, m, h, l, h, m]):
+                rhs[side, blk(i), blk(j, n)] = x
+
+        def row(j, n):
+            h, m, l = split3(z[blk(k), blk(j, n)])
+            r = jnp.dot(a, jnp.concatenate([h, m, h, l, h, m], axis=0), preferred_element_type=F32)
+            put(j, n, r)
+            return r
+
+        z[blk(k), blk(k)] = v
+        put(k, 1, v)
+        for j in range(0, k, 2):
+            n = min(2, k - j)
+            z[blk(k), blk(j, n)] = row(j, n)
+        for j in range(k + 1, NK, 2):
+            n = min(2, NK - j)
+            r = row(j, n)
+            for q in range(n):
+                x = split3(r[:, blk(q)].T)
+                for i, t in enumerate([0, 0, 1, 0, 2, 1]):
+                    lhs[side, blk(j + q), blk(i)] = x[t]
+
+        def reduce(i, m, j, n, side=side):
+            prod = jnp.dot(lhs[side, blk(i, m), :], rhs[side, :, blk(j, n)], preferred_element_type=F32)
+            z[blk(i, m), blk(j, n)] = z[blk(i, m), blk(j, n)] - prod
+
+        def later(*args):
+            pending.append(lambda: reduce(*args))
+
+        if k + 1 < NK:
+            for j in range(0, k + 1, 2):
+                reduce(k + 1, 1, j, min(2, k + 1 - j))
+            for j in range(k + 1, NK, 2):
+                reduce(k + 1, 1, j, min(2, NK - j))
+        for j in range(0, k + 1, 2):
+            for i in range(k + 2, NK, 3):
+                later(i, min(3, NK - i), j, min(2, k + 1 - j), side)
+        for j in range(k + 2, NK, 2):
+            n = min(2, NK - j)
+            for i in range(k + 2, j + 1, 3):
+                later(i, min(3, j + 1 - i), j, n, side)
+            if n == 2:
+                later(j + 1, 1, j + 1, 1, side)
 
 
 def transform_kernel(scal, ga, gb, drive_ref, xa, xb, mean_ref, out_ref, z, dz, vb, lhs, rhs, t, x):
@@ -204,32 +251,38 @@
     rows = lax.broadcasted_iota(jnp.int32, (NB, NB), 0)
     ridge = jnp.where(rows == lax.broadcasted_iota(jnp.int32, (NB, NB), 1), N - 1.0, 0.0)
     zero_core = (rows * 0 + core) == 0
+    for i in range(1, NK):
+        z[blk(i), 0 : i * NB] = jnp.zeros((NB, i * NB), F32)
     for c in range(2):
         for n, (i, d) in enumerate(blocks_of(c)):
             j = i + d
-            a = ga[n * NB : (n + 1) * NB, :]
-            b = gb[n * NB : (n + 1) * NB, :]
-            blk = jnp.where(zero_core, a, b) if c == 0 else jnp.where(zero_core, b, a)
+            a = ga[blk(n), :]
+            b = gb[blk(n), :]
+            g = jnp.where(zero_core, a, b) if c == 0 else jnp.where(zero_core, b, a)
             if d == 0:
-                z[i * NB : (i + 1) * NB, i * NB : (i + 1) * NB] = blk + ridge
+                z[blk(i), blk(i)] = g + ridge
             elif j < NK:
-                z[i * NB : (i + 1) * NB, j * NB : (j + 1) * NB] = blk
+                z[blk(i), blk(j)] = g
             else:
-                z[(j - NK) * NB : (j - NK + 1) * NB, i * NB : (i + 1) * NB] = blk.T
+                z[blk(j - NK), blk(i)] = g.T
     inverse_factor(z, dz, vb, lhs, rhs)
     drive = jnp.concatenate([drive_ref[i : i + 1, :] for i in range(NK)], axis=1)
-
-    def weigh(i, acc):
-        x = z[at(i, 64), :]
-        x = x * jnp.sum(x * drive, axis=1, keepdims=True)
-        for q in range(8):
-            acc = acc + x[q * 8 : (q + 1) * 8]
-        return acc
-
-    weights = jnp.sum(lax.fori_loop(0, N // 64, weigh, jnp.zeros((8, N), F32)), axis=0, keepdims=True)
+    sums = [jnp.zeros((8, NB), F32) for _ in range(NK)]
+    for i in range(NK):
+        width = (i + 1) * NB
+        for h in range(2):
+            y = z[i * NB + 64 * h : i * NB + 64 * h + 64, 0:width]
+            y = y * jnp.sum(y * drive[:, 0:width], axis=1, keepdims=True)
+            for q in range(8):
+                for j in range(i + 1):
+                    sums[j] = sums[j] + y[q * 8 : (q + 1) * 8, blk(j)]
+    weights = jnp.sum(jnp.concatenate(sums, axis=1), axis=0, keepdims=True)
     corr = []
     for i in range(NK):
-        own = (z[at(2 * i + core, 64), :] * math.sqrt(N - 1) + weights).astype(BF)
+        own = z[at(2 * i + core, 64), 0 : (i + 1) * NB] * math.sqrt(N - 1)
+        if i + 1 < NK:
+            own = jnp.concatenate([own, jnp.zeros((64, N - (i + 1) * NB), F32)], axis=1)
+        own = (own + weights).astype(BF)
         t[i * 64 : (i + 1) * 64, :] = own
         corr.append(1.0 - jnp.sum(own.astype(F32), axis=1, keepdims=True))
         x[at(2 * i + core, 64), :] = xa[i]
@@ -250,8 +303,8 @@
             pltpu.VMEM((N, N), F32),
             pltpu.VMEM((NB, 2 * NB), F32),
             pltpu.VMEM((NB, NB), F32),
-            pltpu.VMEM((6 * NB, N), BF),
-            pltpu.VMEM((6 * NB, N), BF),
+            pltpu.VMEM((2, N, 6 * NB), BF),
+            pltpu.VMEM((2, 6 * NB, N), BF),
             pltpu.VMEM((N // 2, N), BF),
             pltpu.VMEM((N, PART), BF),
         ],

time: 161 us -> 147 us (0.913)
  Pallas kernels: 51.7 us -> 38.1 us
    pallas_call x1, Pallas kernels: 47.9 us -> 34.3 us  [transform(): pl.pallas_call(transform_kernel, out_shape=jax.ShapeDtypeStruct((NK, 64,...]
where the time goes in v4:
time: 147 us; the launch traced here: 146 us
  blocking collectives  96 us (65%)
  Pallas kernels  38.1 us (26%)
  starting transfers between devices  7.12 us (5%)
  waiting for transfers between devices  2.47 us (2%)
  local copies, waits for them, and re-layouts  2.33 us (2%)
    pallas_call x1, Pallas kernels, transform(): pl.pallas_call(transform_kernel, out_shape=jax.ShapeDtypeStruct((NK, 64,...  34.3 us
    all_to_all x2, blocking collectives, gather(): lax.all_to_all(jnp.broadcast_to(x[None], (size, *x.shape)), axes, 0, 0, t...  27.3 us
    all_to_all x1, blocking collectives, per_device(): part = jnp.sum(lax.all_to_all(part, PLANE, 0, 0, tiled=True), axis=0)  21.3 us
    all_to_all x1, blocking collectives, per_device(): xa = lax.all_to_all(background_samples.reshape(64, NK, PART), CHIPS, 1, 0)  18 us
    all_to_all x1, blocking collectives, per_device(): part = jnp.sum(lax.all_to_all(part, ('z',), 0, 0, tiled=True), axis=0)  15.6 us
    all_to_all x1, blocking collectives, per_device(): return lax.all_to_all(out, CHIPS, 0, 1).reshape(64, CELLS)  13.9 us
    ppermute x2, starting transfers between devices, swap(): return lax.ppermute(x, 'core', [(0, 1), (1, 0)])  7.12 us
  transfers between devices with their start and end apart: 2, of which 1 were waited for; matrix products, arithmetic and copies ran while one was open for 0% of the time, Pallas kernels for 1%

profile of v4, /device:TPU:1, one launch (start us, length us, event | category | flops | bytes accessed | tf_op | source)
XLA Modules:
  0.0 146.3 jit_solution(9731208597314419404)
XLA Ops:
  0.0 1.2 copy.13
  1.2 0.0 copy-start
  1.2 0.0 copy-start.1
  1.2 0.0 copy-start.2
  1.3 0.2 copy.10
  1.4 18.0 %all_to_all.50 = bf16[1,64,8,512]{3,1,0,2:T(8,128)(2,1)S(1)} all-to-all(bf16[1,64,8,512]{3,1,0,2:T(8,128)(2,1)S(1)} %copy.10), channel_id=1, replica_groups=mesh['yh'=2,'x'=4,'core'=2,'z'=8,'yl'=2] {'yh','x'}, dimensions={2} | all-to-all | bytes 1048576 | tf_op jit(solution)/shard_map/all_to_all | solution.py:332
  19.4 1.9 %collective-permute-start = (bf16[8,64,512]{2,1,0:T(8,128)(2,1)S(1)}, bf16[8,64,512]{2,1,0:T(8,128)(2,1)S(1)}, u32[]{:S(2)}, u32[]{:S(2)}) collective-permute-start(bf16[8,64,512]{2,1,0:T(8,128)(2,1)S(1)} %bitcast.32), channel_id=1, source_target_pairs={{0,16},{16,0},{1,17},{17,1},{2,18},{18,2},{3,19},{19,3},{4,20},{20... | collective-permute-start | bytes 1572872 | tf_op jit(solution)/shard_map/ppermute | solution.py:318
  21.2 0.1 pad_add_fusion.scal
  21.3 0.0 copy-done
  21.3 0.0 copy-done.1
  21.3 0.0 copy-done.2
  21.3 1.8 %obs_sums.1.ws_ref = f32[8,512]{1,0:T(8,128)S(1)} custom-call(s32[3]{0:T(128)S(1)} %pad_add_fusion.scal, s32[64,128]{1,0:T(8,128)S(1)} %bitcast.36, f32[64,128]{1,0:T(8,128)S(1)} %bitcast.37, f32[64,128]{1,0:T(8,128)S(1)} %bitcast.38), custom_call_target="tpu_custom_call" | custom-call | flops 67108864 | bytes 200000 | tf_op jit(solution)/shard_map/obs_sums/pallas_call | solution.py:69
  23.1 0.0 collective-permute-done.xb
  23.1 2.0 %gram_part.1 = (f32[16,152,128]{2,1,0:T(8,128)S(1)}, f32[8,512]{1,0:T(8,128)S(1)}) custom-call(s32[3]{0:T(128)S(1)} %pad_add_fusion.scal, f32[8,512]{1,0:T(8,128)S(1)} %obs_sums.1.ws_ref, bf16[8,64,512]{2,1,0:T(8,128)(2,1)S(1)} %bitcast.33, bf16[8,64,512]{2,1,0:T(8,128)(2,1)S(1)} %collective-permute-done.xb), custom_call_target="tpu_custom_call" | custom-call | flops 301989888 | bytes 3145728 | tf_op jit(solution)/shard_map/gram_part/pallas_call | solution.py:116
  25.2 21.3 %all_to_all.51 = f32[16,152,128]{2,1,0:T(8,128)S(1)} all-to-all(f32[16,152,128]{2,1,0:T(8,128)S(1)} %get-tuple-element.7), channel_id=1, replica_groups=mesh['yh'=2,'x'=4,'core'=2,'z'=8,'yl'=2] {'yh','x','yl'}, dimensions={0} | all-to-all | bytes 2490368 | tf_op jit(solution)/shard_map/all_to_all | solution.py:336
  46.5 0.1 reduce_sum.18
  46.6 15.6 %all_to_all.52 = f32[8,24,128]{2,1,0:T(8,128)S(1)} all-to-all(f32[8,24,128]{2,1,0:T(8,128)S(1)} %bitcast.42), channel_id=1, replica_groups=mesh['yh'=2,'x'=4,'core'=2,'z'=8,'yl'=2] {'z'}, dimensions={0} | all-to-all | bytes 196608 | tf_op jit(solution)/shard_map/all_to_all | solution.py:338
  62.2 10.0 %all_to_all.53 = f32[8,24,128]{2,1,0:T(8,128)S(1)} all-to-all(f32[8,24,128]{2,1,0:T(8,128)S(1)} %broadcast_in_dim.8), channel_id=1, replica_groups=mesh['yh'=2,'x'=4,'core'=2,'z'=8,'yl'=2] {'z'}, dimensions={0} | all-to-all | bytes 196608 | tf_op jit(solution)/shard_map/all_to_all | solution.py:326
  72.1 0.1 broadcast_in_dim.19
  72.2 17.3 %all_to_all.54 = f32[16,144,128]{2,1,0:T(8,128)S(1)} all-to-all(f32[16,144,128]{2,1,0:T(8,128)S(1)} %broadcast_in_dim.19), channel_id=1, replica_groups=mesh['yh'=2,'x'=4,'core'=2,'z'=8,'yl'=2] {'yh','x','yl'}, dimensions={0} | all-to-all | bytes 2359296 | tf_op jit(solution)/shard_map/all_to_all | solution.py:326
  89.6 5.3 %collective-permute-start.1 = (f32[2304,128]{1,0:T(8,128)S(1)}, f32[2304,128]{1,0:T(8,128)S(1)}, u32[]{:S(2)}, u32[]{:S(2)}) collective-permute-start(f32[2304,128]{1,0:T(8,128)S(1)} %bitcast.30), channel_id=1, source_target_pairs={{0,16},{16,0},{1,17},{17,1},{2,18},{18,2},{3,19},{19,3},{4,20},{20... | collective-permute-start | bytes 3538952 | tf_op jit(solution)/shard_map/ppermute | solution.py:318
  94.8 2.5 %collective-permute-done.1.gb = f32[2304,128]{1,0:T(8,128)S(1)} collective-permute-done((f32[2304,128]{1,0:T(8,128)S(1)}, f32[2304,128]{1,0:T(8,128)S(1)}, u32[]{:S(2)}, u32[]{:S(2)}) %collective-permute-start.1) | collective-permute-done | bytes 1179680 | tf_op jit(solution)/shard_map/ppermute | solution.py:318
  97.3 34.3 %transform.1 = bf16[8,64,512]{2,1,0:T(8,128)(2,1)S(1)} custom-call(s32[3]{0:T(128)S(1)} %pad_add_fusion.scal, f32[2304,128]{1,0:T(8,128)S(1)} %bitcast.31, f32[2304,128]{1,0:T(8,128)S(1)} %collective-permute-done.1.gb, f32[8,128]{1,0:T(8,128)S(1)} %slice.10.drive_ref, bf16[8,64,512]{2,1,0:T(8,128)(2,1)S(1)} %bitcast.34, ...), custom_call_target="tpu_custom_call" | custom-call | flops 10000000000 | bytes 4194304 | tf_op jit(solution)/shard_map/transform/pallas_call | solution.py:297
  131.6 13.9 %all_to_all.55 = bf16[8,64,1,512]{3,1,2,0:T(8,128)(2,1)S(1)} all-to-all(bf16[8,64,1,512]{3,1,2,0:T(8,128)(2,1)S(1)} %bitcast.35), channel_id=1, replica_groups=mesh['yh'=2,'x'=4,'core'=2,'z'=8,'yl'=2] {'yh','x'}, dimensions={0} | all-to-all | bytes 1048576 | tf_op jit(solution)/shard_map/all_to_all | solution.py:343
  145.5 0.8 copy.14
  (5 shorter events, 0.0 us)
Async XLA Ops:
  1.2 20.1 %copy-start = (s32[8192]{0:T(1024)S(1)}, s32[8192]{0:T(1024)}, u32[]{:S(2)}) copy-start(s32[8192]{0:T(1024)} %param.5) | copy-start | bytes 98308
  1.2 20.1 %copy-start.1 = (f32[8192]{0:T(1024)S(1)}, f32[8192]{0:T(1024)}, u32[]{:S(2)}) copy-start(f32[8192]{0:T(1024)} %param.6) | copy-start | bytes 98308
  1.2 20.1 %copy-start.2 = (f32[8192]{0:T(1024)S(1)}, f32[8192]{0:T(1024)}, u32[]{:S(2)}) copy-start(f32[8192]{0:T(1024)} %param.7) | copy-start | bytes 98308
  19.4 3.8 %collective-permute-start = (bf16[8,64,512]{2,1,0:T(8,128)(2,1)S(1)}, bf16[8,64,512]{2,1,0:T(8,128)(2,1)S(1)}, u32[]{:S(2)}, u32[]{:S(2)}) collective-permute-start(bf16[8,64,512]{2,1,0:T(8,128)(2,1)S(1)} %bitcast.32), channel_id=1, source_target_pairs={{0,16},{16,0},{1,17},{17,1},{2,18},{18,2},{3,19},{19,3},{4,20},{20... | collective-permute-start | bytes 1572872 | tf_op jit(solution)/shard_map/ppermute | solution.py:318
  89.6 7.7 %collective-permute-start.1 = (f32[2304,128]{1,0:T(8,128)S(1)}, f32[2304,128]{1,0:T(8,128)S(1)}, u32[]{:S(2)}, u32[]{:S(2)}) collective-permute-start(f32[2304,128]{1,0:T(8,128)S(1)} %bitcast.30), channel_id=1, source_target_pairs={{0,16},{16,0},{1,17},{17,1},{2,18},{18,2},{3,19},{19,3},{4,20},{20... | collective-permute-start | bytes 3538952 | tf_op jit(solution)/shard_map/ppermute | solution.py:318

commit v5 on v4

--- a/solution.py
+++ b/solution.py
@@ -125,14 +125,17 @@
     )(scal, ws, xa, xb)
 
 
-def diag_inverse(dz, vout, thunks):
+def diag_inverse(dz, vout, eb, thunks):
     steps = NB // SB
     done = 0
+    now = dz[0:SB, 0:NB]
     for j in range(steps):
         r0 = j * SB
         rs = [jnp.broadcast_to(dz[r0 + p : r0 + p + 1, 0:NB], (SB, NB)) for p in range(SB)]
         rw = [jnp.broadcast_to(dz[r0 + p : r0 + p + 1, NB : 2 * NB], (SB, NB)) for p in range(SB)]
-        e = [[jnp.broadcast_to(rs[q][:, r0 + p : r0 + p + 1], (SB, NB)) for p in range(q + 1)] for q in range(SB)]
+        for p in range(SB):
+            eb[p] = jnp.broadcast_to(now[:, r0 + p : r0 + p + 1], (SB, NB))
+        e = [[jnp.broadcast_to(eb[p, q : q + 1, :], (SB, NB)) for p in range(q + 1)] for q in range(SB)]
         c = {}
         for g in range(j + 1, steps):
             below = dz[g * SB : (g + 1) * SB, 0:NB]
@@ -146,6 +149,7 @@
                 dw = dw - c[g][p] * w[p]
             dz[g * SB : (g + 1) * SB, 0:NB] = ds
             dz[g * SB : (g + 1) * SB, NB : 2 * NB] = dw
+            return ds
 
         following = range(j + 1, min(j + 2, steps))
         f, r = [], []
@@ -167,7 +171,7 @@
         for p in range(SB):
             vout[r0 + p : r0 + p + 1, :] = rw[p][0:1, :]
         for g in following:
-            subtract(g, rs, rw)
+            now = subtract(g, rs, rw)
         if j + 2 < steps:
             for v in (rs, rw):
                 for p in range(SB - 1, -1, -1):
@@ -185,68 +189,78 @@
     return slice(i * NB, (i + n) * NB)
 
 
-def inverse_factor(z, dz, vb, lhs, rhs):
+def inverse_factor(z, dz, vb, eb, ab, lhs, rhs):
     rows = lax.broadcasted_iota(jnp.int32, (NB, NB), 0)
     eye = jnp.where(rows == lax.broadcasted_iota(jnp.int32, (NB, NB), 1), 1.0, 0.0)
+
+    def put(side, j, n, r):
+        h, m, l = split3(r)
+        for i, x in enumerate([h, m, h, l, h, m]):
+            rhs[side, blk(i), blk(j, n)] = x
+
+    def own(k):
+        v = vb[k % 2]
+        z[blk(k), blk(k)] = v
+        put(k % 2, k, 1, v)
+
+    def row(k, j, n):
+        side = k % 2
+        h, m, l = split3(z[blk(k), blk(j, n)])
+        r = jnp.dot(ab[side], jnp.concatenate([h, m, h, l, h, m], axis=0), preferred_element_type=F32)
+        put(side, j, n, r)
+        if j < k:
+            z[blk(k), blk(j, n)] = r
+            return
+        for q in range(n):
+            x = split3(r[:, blk(q)].T)
+            for i, t in enumerate([0, 0, 1, 0, 2, 1]):
+                lhs[side, blk(j + q), blk(i)] = x[t]
+
+    def reduce(side, i, m, j, n):
+        prod = jnp.dot(lhs[side, blk(i, m), :], rhs[side, :, blk(j, n)], preferred_element_type=F32)
+        z[blk(i, m), blk(j, n)] = z[blk(i, m), blk(j, n)] - prod
+
     pending = []
+
+    def later(f, *args):
+        pending.append(lambda: f(*args))
+
     for k in range(NK):
+        side = k % 2
         dz[:, 0:NB] = z[blk(k), blk(k)]
         dz[:, NB : 2 * NB] = eye
-        diag_inverse(dz, vb, pending)
-        pending = []
-        v = vb[...]
-        side = k % 2
-        vh, vm, vl = split3(v)
-        a = jnp.concatenate([vh, vh, vm, vh, vl, vm], axis=1)
-
-        def put(j, n, r):
-            h, m, l = split3(r)
-            for i, x in enumerate([h, m, h, l, h, m]):
-                rhs[side, blk(i), blk(j, n)] = x
-
-        def row(j, n):
-            h, m, l = split3(z[blk(k), blk(j, n)])
-            r = jnp.dot(a, jnp.concatenate([h, m, h, l, h, m], axis=0), preferred_element_type=F32)
-            put(j, n, r)
-            return r
-
-        z[blk(k), blk(k)] = v
-        put(k, 1, v)
+        diag_inverse(dz, vb.at[side], eb.at[side], pending)
+        pending.clear()
+        h, m, l = split3(vb[side])
+        for i, x in enumerate([h, h, m, h, l, m]):
+            ab[side, :, blk(i)] = x
+        later(own, k)
+        if k + 1 < NK:
+            row(k, k + 1, 1)
+            reduce(side, k + 1, 1, k + 1, 1)
         for j in range(0, k, 2):
-            n = min(2, k - j)
-            z[blk(k), blk(j, n)] = row(j, n)
-        for j in range(k + 1, NK, 2):
-            n = min(2, NK - j)
-            r = row(j, n)
-            for q in range(n):
-                x = split3(r[:, blk(q)].T)
-                for i, t in enumerate([0, 0, 1, 0, 2, 1]):
-                    lhs[side, blk(j + q), blk(i)] = x[t]
-
-        def reduce(i, m, j, n, side=side):
-            prod = jnp.dot(lhs[side, blk(i, m), :], rhs[side, :, blk(j, n)], preferred_element_type=F32)
-            z[blk(i, m), blk(j, n)] = z[blk(i, m), blk(j, n)] - prod
-
-        def later(*args):
-            pending.append(lambda: reduce(*args))
-
+            later(row, k, j, min(2, k - j))
+        for j in range(k + 2, NK, 2):
+            later(row, k, j, min(2, NK - j))
         if k + 1 < NK:
             for j in range(0, k + 1, 2):
-                reduce(k + 1, 1, j, min(2, k + 1 - j))
-            for j in range(k + 1, NK, 2):
-                reduce(k + 1, 1, j, min(2, NK - j))
+                later(reduce, side, k + 1, 1, j, min(2, k + 1 - j))
+            for j in range(k + 2, NK, 2):
+                later(reduce, side, k + 1, 1, j, min(2, NK - j))
         for j in range(0, k + 1, 2):
             for i in range(k + 2, NK, 3):
-                later(i, min(3, NK - i), j, min(2, k + 1 - j), side)
+                later(reduce, side, i, min(3, NK - i), j, min(2, k + 1 - j))
         for j in range(k + 2, NK, 2):
             n = min(2, NK - j)
             for i in range(k + 2, j + 1, 3):
-                later(i, min(3, j + 1 - i), j, n, side)
+                later(reduce, side, i, min(3, j + 1 - i), j, n)
             if n == 2:
-                later(j + 1, 1, j + 1, 1, side)
-
-
-def transform_kernel(scal, ga, gb, drive_ref, xa, xb, mean_ref, out_ref, z, dz, vb, lhs, rhs, t, x):
+                later(reduce, side, j + 1, 1, j + 1, 1)
+    for f in pending:
+        f()
+
+
+def transform_kernel(scal, ga, gb, drive_ref, xa, xb, mean_ref, out_ref, z, dz, vb, eb, ab, lhs, rhs, t, x):
     core = scal[2]
     rows = lax.broadcasted_iota(jnp.int32, (NB, NB), 0)
     ridge = jnp.where(rows == lax.broadcasted_iota(jnp.int32, (NB, NB), 1), N - 1.0, 0.0)
@@ -265,7 +279,7 @@
                 z[blk(i), blk(j)] = g
             else:
                 z[blk(j - NK), blk(i)] = g.T
-    inverse_factor(z, dz, vb, lhs, rhs)
+    inverse_factor(z, dz, vb, eb, ab, lhs, rhs)
     drive = jnp.concatenate([drive_ref[i : i + 1, :] for i in range(NK)], axis=1)
     sums = [jnp.zeros((8, NB), F32) for _ in range(NK)]
     for i in range(NK):
@@ -302,7 +316,9 @@
         scratch_shapes=[
             pltpu.VMEM((N, N), F32),
             pltpu.VMEM((NB, 2 * NB), F32),
-            pltpu.VMEM((NB, NB), F32),
+            pltpu.VMEM((2, NB, NB), F32),
+            pltpu.VMEM((2, SB, SB, NB), F32),
+            pltpu.VMEM((2, NB, 6 * NB), BF),
             pltpu.VMEM((2, N, 6 * NB), BF),
             pltpu.VMEM((2, 6 * NB, N), BF),
             pltpu.VMEM((N // 2, N), BF),
@@ -334,9 +350,8 @@
     ws = obs_sums(scal, sensor_cell_offsets, sensor_data, sensor_sigma_list)
     part, mean = gram_part(scal, ws, xa, xb)
     part = jnp.sum(lax.all_to_all(part, PLANE, 0, 0, tiled=True), axis=0)
-    part = jnp.pad(part, ((0, 40), (0, 0))).reshape(8, 24, NB)
-    part = jnp.sum(lax.all_to_all(part, ("z",), 0, 0, tiled=True), axis=0)
-    part = gather(part, ("z",), 8).reshape(192, NB)
+    for step in (1, 2, 4):
+        part = part + lax.ppermute(part, "z", [(i, i ^ step) for i in range(8)])
     ga = gather(part[:GROWS], PLANE, 16).reshape(16 * GROWS, NB)
     gb = swap(ga)
     out = transform(scal, ga, gb, part[GROWS : GROWS + 8], xa, xb, mean)

time: 147 us -> 137 us (0.932)
  blocking collectives: 96 us -> 69.8 us
  starting transfers between devices: 7.12 us -> 19.8 us
  waiting for transfers between devices: 2.47 us -> 7.84 us
    all_to_all x1 -> x0, blocking collectives: 15.6 us -> none  [per_device(): part = jnp.sum(lax.all_to_all(part, ('z',), 0, 0, tiled=True), axis=0)]
    ppermute x0 -> x3, starting transfers between devices: none -> 11.8 us  [per_device(): part = part + lax.ppermute(part, 'z', [(i, i ^ step) for i in range(8)])]
    all_to_all x2 -> x1, blocking collectives: 27.3 us -> 16.4 us  [gather(): lax.all_to_all(jnp.broadcast_to(x[None], (size, *x.shape)), axes, 0, 0, t...]
    ppermute x0 -> x3, waiting for transfers between devices: none -> 5.36 us  [per_device(): part = part + lax.ppermute(part, 'z', [(i, i ^ step) for i in range(8)])]
  transfers between devices with their start and end apart: 2 -> 5, of which waited for: 1 -> 4; matrix products, arithmetic and copies ran while one was open for 0% -> 0% of each run, Pallas kernels for 1% -> 1%
where the time goes in v5:
time: 137 us
  blocking collectives  69.8 us (51%)
  Pallas kernels  37 us (27%)
  starting transfers between devices  19.8 us (14%)
  waiting for transfers between devices  7.84 us (6%)
  local copies, waits for them, and re-layouts  2.31 us (2%)
    pallas_call x1, Pallas kernels, transform(): pl.pallas_call(transform_kernel, out_shape=jax.ShapeDtypeStruct((NK, 64,...  33.1 us
    all_to_all x1, blocking collectives, per_device(): part = jnp.sum(lax.all_to_all(part, PLANE, 0, 0, tiled=True), axis=0)  21.3 us
    all_to_all x1, blocking collectives, per_device(): xa = lax.all_to_all(background_samples.reshape(64, NK, PART), CHIPS, 1, 0)  18 us
    all_to_all x1, blocking collectives, gather(): lax.all_to_all(jnp.broadcast_to(x[None], (size, *x.shape)), axes, 0, 0, t...  16.4 us
    all_to_all x1, blocking collectives, per_device(): return lax.all_to_all(out, CHIPS, 0, 1).reshape(64, CELLS)  14 us
    ppermute x3, starting transfers between devices, per_device(): part = part + lax.ppermute(part, 'z', [(i, i ^ step) for i in range(8)])  11.8 us
    ppermute x2, starting transfers between devices, swap(): return lax.ppermute(x, 'core', [(0, 1), (1, 0)])  8.02 us
    ppermute x3, waiting for transfers between devices, per_device(): part = part + lax.ppermute(part, 'z', [(i, i ^ step) for i in range(8)])  5.36 us
  transfers between devices with their start and end apart: 5, of which 4 were waited for; matrix products, arithmetic and copies ran while one was open for 0% of the time, Pallas kernels for 1%

profile of v5, /device:TPU:1, one launch (start us, length us, event | category | flops | bytes accessed | tf_op | source)
XLA Modules:
  0.0 137.0 jit_solution(2513869321354133796)
XLA Ops:
  0.0 1.2 copy.10
  1.2 0.0 copy-start
  1.2 0.0 copy-start.1
  1.2 0.0 copy-start.2
  1.3 0.2 copy.7
  1.4 18.0 %all_to_all.40 = bf16[1,64,8,512]{3,1,0,2:T(8,128)(2,1)S(1)} all-to-all(bf16[1,64,8,512]{3,1,0,2:T(8,128)(2,1)S(1)} %copy.7), channel_id=1, replica_groups=mesh['yh'=2,'x'=4,'core'=2,'z'=8,'yl'=2] {'yh','x'}, dimensions={2} | all-to-all | bytes 1048576 | tf_op jit(solution)/shard_map/all_to_all | solution.py:348
  19.4 1.9 %collective-permute-start = (bf16[8,64,512]{2,1,0:T(8,128)(2,1)S(1)}, bf16[8,64,512]{2,1,0:T(8,128)(2,1)S(1)}, u32[]{:S(2)}, u32[]{:S(2)}) collective-permute-start(bf16[8,64,512]{2,1,0:T(8,128)(2,1)S(1)} %bitcast.29), channel_id=1, source_target_pairs={{0,16},{16,0},{1,17},{17,1},{2,18},{18,2},{3,19},{19,3},{4,20},{20... | collective-permute-start | bytes 1572872 | tf_op jit(solution)/shard_map/ppermute | solution.py:334
  21.2 0.1 pad_add_fusion.scal
  21.3 0.0 copy-done
  21.3 0.0 copy-done.1
  21.3 0.0 copy-done.2
  21.3 1.8 %obs_sums.1.ws_ref = f32[8,512]{1,0:T(8,128)S(1)} custom-call(s32[3]{0:T(128)S(1)} %pad_add_fusion.scal, s32[64,128]{1,0:T(8,128)S(1)} %bitcast.33, f32[64,128]{1,0:T(8,128)S(1)} %bitcast.34, f32[64,128]{1,0:T(8,128)S(1)} %bitcast.35), custom_call_target="tpu_custom_call" | custom-call | flops 67108864 | bytes 200000 | tf_op jit(solution)/shard_map/obs_sums/pallas_call | solution.py:69
  23.1 0.0 collective-permute-done.xb
  23.1 2.0 %gram_part.1 = (f32[16,152,128]{2,1,0:T(8,128)S(1)}, f32[8,512]{1,0:T(8,128)S(1)}) custom-call(s32[3]{0:T(128)S(1)} %pad_add_fusion.scal, f32[8,512]{1,0:T(8,128)S(1)} %obs_sums.1.ws_ref, bf16[8,64,512]{2,1,0:T(8,128)(2,1)S(1)} %bitcast.30, bf16[8,64,512]{2,1,0:T(8,128)(2,1)S(1)} %collective-permute-done.xb), custom_call_target="tpu_custom_call" | custom-call | flops 301989888 | bytes 3145728 | tf_op jit(solution)/shard_map/gram_part/pallas_call | solution.py:116
  25.2 21.3 %all_to_all.41 = f32[16,152,128]{2,1,0:T(8,128)S(1)} all-to-all(f32[16,152,128]{2,1,0:T(8,128)S(1)} %get-tuple-element.7), channel_id=1, replica_groups=mesh['yh'=2,'x'=4,'core'=2,'z'=8,'yl'=2] {'yh','x','yl'}, dimensions={0} | all-to-all | bytes 2490368 | tf_op jit(solution)/shard_map/all_to_all | solution.py:352
  46.5 0.1 reduce_sum.9
  46.6 1.7 %collective-permute-start.1 = (f32[152,128]{1,0:T(8,128)S(1)}, f32[152,128]{1,0:T(8,128)S(1)}, u32[]{:S(2)}, u32[]{:S(2)}) collective-permute-start(f32[152,128]{1,0:T(8,128)S(1)} %reduce_sum.9), channel_id=1, source_target_pairs={{0,2},{2,0},{4,6},{6,4},{8,10},{10,8},{12,14},{14,12},{1,3},{3,1},... | collective-permute-start | bytes 233480 | tf_op jit(solution)/shard_map/ppermute | solution.py:354
  48.3 1.8 %collective-permute-done.1 = f32[152,128]{1,0:T(8,128)S(1)} collective-permute-done((f32[152,128]{1,0:T(8,128)S(1)}, f32[152,128]{1,0:T(8,128)S(1)}, u32[]{:S(2)}, u32[]{:S(2)}) %collective-permute-start.1) | collective-permute-done | bytes 77856 | tf_op jit(solution)/shard_map/ppermute | solution.py:354
  50.1 3.1 %collective-permute-start.2 = (f32[152,128]{1,0:T(8,128)S(1)}, f32[152,128]{1,0:T(8,128)S(1)}, u32[]{:S(2)}, u32[]{:S(2)}) collective-permute-start(f32[152,128]{1,0:T(8,128)S(1)} %add.9), channel_id=1, source_target_pairs={{0,4},{2,6},{4,0},{6,2},{8,12},{10,14},{12,8},{14,10},{1,5},{3,7},... | collective-permute-start | bytes 233480 | tf_op jit(solution)/shard_map/ppermute | solution.py:354
  53.2 1.8 %collective-permute-done.2 = f32[152,128]{1,0:T(8,128)S(1)} collective-permute-done((f32[152,128]{1,0:T(8,128)S(1)}, f32[152,128]{1,0:T(8,128)S(1)}, u32[]{:S(2)}, u32[]{:S(2)}) %collective-permute-start.2) | collective-permute-done | bytes 77856 | tf_op jit(solution)/shard_map/ppermute | solution.py:354
  55.0 7.0 %collective-permute-start.3 = (f32[152,128]{1,0:T(8,128)S(1)}, f32[152,128]{1,0:T(8,128)S(1)}, u32[]{:S(2)}, u32[]{:S(2)}) collective-permute-start(f32[152,128]{1,0:T(8,128)S(1)} %add.10), channel_id=1, source_target_pairs={{0,8},{2,10},{4,12},{6,14},{8,0},{10,2},{12,4},{14,6},{1,9},{3,11}... | collective-permute-start | bytes 233480 | tf_op jit(solution)/shard_map/ppermute | solution.py:354
  62.0 1.8 %collective-permute-done.3 = f32[152,128]{1,0:T(8,128)S(1)} collective-permute-done((f32[152,128]{1,0:T(8,128)S(1)}, f32[152,128]{1,0:T(8,128)S(1)}, u32[]{:S(2)}, u32[]{:S(2)}) %collective-permute-start.3) | collective-permute-done | bytes 77856 | tf_op jit(solution)/shard_map/ppermute | solution.py:354
  63.8 0.1 broadcast_in_dim.4
  63.9 16.4 %all_to_all.42 = f32[16,144,128]{2,1,0:T(8,128)S(1)} all-to-all(f32[16,144,128]{2,1,0:T(8,128)S(1)} %broadcast_in_dim.4), channel_id=1, replica_groups=mesh['yh'=2,'x'=4,'core'=2,'z'=8,'yl'=2] {'yh','x','yl'}, dimensions={0} | all-to-all | bytes 2359296 | tf_op jit(solution)/shard_map/all_to_all | solution.py:342
  80.3 6.2 %collective-permute-start.4 = (f32[2304,128]{1,0:T(8,128)S(1)}, f32[2304,128]{1,0:T(8,128)S(1)}, u32[]{:S(2)}, u32[]{:S(2)}) collective-permute-start(f32[2304,128]{1,0:T(8,128)S(1)} %bitcast.27), channel_id=1, source_target_pairs={{0,16},{16,0},{1,17},{17,1},{2,18},{18,2},{3,19},{19,3},{4,20},{20... | collective-permute-start | bytes 3538952 | tf_op jit(solution)/shard_map/ppermute | solution.py:334
  86.5 2.5 %collective-permute-done.4.gb = f32[2304,128]{1,0:T(8,128)S(1)} collective-permute-done((f32[2304,128]{1,0:T(8,128)S(1)}, f32[2304,128]{1,0:T(8,128)S(1)}, u32[]{:S(2)}, u32[]{:S(2)}) %collective-permute-start.4) | collective-permute-done | bytes 1179680 | tf_op jit(solution)/shard_map/ppermute | solution.py:334
  89.0 33.1 %transform.1 = bf16[8,64,512]{2,1,0:T(8,128)(2,1)S(1)} custom-call(s32[3]{0:T(128)S(1)} %pad_add_fusion.scal, f32[2304,128]{1,0:T(8,128)S(1)} %bitcast.28, f32[2304,128]{1,0:T(8,128)S(1)} %collective-permute-done.4.gb, f32[8,128]{1,0:T(8,128)S(1)} %slice.9.drive_ref, bf16[8,64,512]{2,1,0:T(8,128)(2,1)S(1)} %bitcast.31, ...), custom_call_target="tpu_custom_call" | custom-call | flops 10000000000 | bytes 4194304 | tf_op jit(solution)/shard_map/transform/pallas_call | solution.py:311
  122.1 14.0 %all_to_all.43 = bf16[8,64,1,512]{3,1,2,0:T(8,128)(2,1)S(1)} all-to-all(bf16[8,64,1,512]{3,1,2,0:T(8,128)(2,1)S(1)} %bitcast.32), channel_id=1, replica_groups=mesh['yh'=2,'x'=4,'core'=2,'z'=8,'yl'=2] {'yh','x'}, dimensions={0} | all-to-all | bytes 1048576 | tf_op jit(solution)/shard_map/all_to_all | solution.py:358
  136.1 0.8 copy.11
  (5 shorter events, 0.0 us)
Async XLA Ops:
  1.2 20.1 %copy-start = (s32[8192]{0:T(1024)S(1)}, s32[8192]{0:T(1024)}, u32[]{:S(2)}) copy-start(s32[8192]{0:T(1024)} %param.5) | copy-start | bytes 98308
  1.2 20.1 %copy-start.1 = (f32[8192]{0:T(1024)S(1)}, f32[8192]{0:T(1024)}, u32[]{:S(2)}) copy-start(f32[8192]{0:T(1024)} %param.6) | copy-start | bytes 98308
  1.2 20.1 %copy-start.2 = (f32[8192]{0:T(1024)S(1)}, f32[8192]{0:T(1024)}, u32[]{:S(2)}) copy-start(f32[8192]{0:T(1024)} %param.7) | copy-start | bytes 98308
  19.4 3.8 %collective-permute-start = (bf16[8,64,512]{2,1,0:T(8,128)(2,1)S(1)}, bf16[8,64,512]{2,1,0:T(8,128)(2,1)S(1)}, u32[]{:S(2)}, u32[]{:S(2)}) collective-permute-start(bf16[8,64,512]{2,1,0:T(8,128)(2,1)S(1)} %bitcast.29), channel_id=1, source_target_pairs={{0,16},{16,0},{1,17},{17,1},{2,18},{18,2},{3,19},{19,3},{4,20},{20... | collective-permute-start | bytes 1572872 | tf_op jit(solution)/shard_map/ppermute | solution.py:334
  46.6 3.5 %collective-permute-start.1 = (f32[152,128]{1,0:T(8,128)S(1)}, f32[152,128]{1,0:T(8,128)S(1)}, u32[]{:S(2)}, u32[]{:S(2)}) collective-permute-start(f32[152,128]{1,0:T(8,128)S(1)} %reduce_sum.9), channel_id=1, source_target_pairs={{0,2},{2,0},{4,6},{6,4},{8,10},{10,8},{12,14},{14,12},{1,3},{3,1},... | collective-permute-start | bytes 233480 | tf_op jit(solution)/shard_map/ppermute | solution.py:354
  50.1 4.9 %collective-permute-start.2 = (f32[152,128]{1,0:T(8,128)S(1)}, f32[152,128]{1,0:T(8,128)S(1)}, u32[]{:S(2)}, u32[]{:S(2)}) collective-permute-start(f32[152,128]{1,0:T(8,128)S(1)} %add.9), channel_id=1, source_target_pairs={{0,4},{2,6},{4,0},{6,2},{8,12},{10,14},{12,8},{14,10},{1,5},{3,7},... | collective-permute-start | bytes 233480 | tf_op jit(solution)/shard_map/ppermute | solution.py:354
  55.0 8.8 %collective-permute-start.3 = (f32[152,128]{1,0:T(8,128)S(1)}, f32[152,128]{1,0:T(8,128)S(1)}, u32[]{:S(2)}, u32[]{:S(2)}) collective-permute-start(f32[152,128]{1,0:T(8,128)S(1)} %add.10), channel_id=1, source_target_pairs={{0,8},{2,10},{4,12},{6,14},{8,0},{10,2},{12,4},{14,6},{1,9},{3,11}... | collective-permute-start | bytes 233480 | tf_op jit(solution)/shard_map/ppermute | solution.py:354
  80.3 8.6 %collective-permute-start.4 = (f32[2304,128]{1,0:T(8,128)S(1)}, f32[2304,128]{1,0:T(8,128)S(1)}, u32[]{:S(2)}, u32[]{:S(2)}) collective-permute-start(f32[2304,128]{1,0:T(8,128)S(1)} %bitcast.27), channel_id=1, source_target_pairs={{0,16},{16,0},{1,17},{17,1},{2,18},{18,2},{3,19},{19,3},{4,20},{20... | collective-permute-start | bytes 3538952 | tf_op jit(solution)/shard_map/ppermute | solution.py:334

commit v6 on v5

--- a/solution.py
+++ b/solution.py
@@ -350,7 +350,7 @@
     ws = obs_sums(scal, sensor_cell_offsets, sensor_data, sensor_sigma_list)
     part, mean = gram_part(scal, ws, xa, xb)
     part = jnp.sum(lax.all_to_all(part, PLANE, 0, 0, tiled=True), axis=0)
-    for step in (1, 2, 4):
+    for step in (1, 2, 7):
         part = part + lax.ppermute(part, "z", [(i, i ^ step) for i in range(8)])
     ga = gather(part[:GROWS], PLANE, 16).reshape(16 * GROWS, NB)
     gb = swap(ga)

time: 137 us -> 137 us (level)
  starting transfers between devices: 19.8 us -> 17.8 us
where the time goes in v6:
time: 137 us; the launch traced here: 136 us
  blocking collectives  70.6 us (52%)
  Pallas kernels  36.9 us (27%)
  starting transfers between devices  17.8 us (13%)
  waiting for transfers between devices  8.43 us (6%)
  local copies, waits for them, and re-layouts  2.31 us (2%)
    pallas_call x1, Pallas kernels, transform(): pl.pallas_call(transform_kernel, out_shape=jax.ShapeDtypeStruct((NK, 64,...  33.1 us
    all_to_all x1, blocking collectives, per_device(): part = jnp.sum(lax.all_to_all(part, PLANE, 0, 0, tiled=True), axis=0)  21.3 us
    all_to_all x1, blocking collectives, per_device(): xa = lax.all_to_all(background_samples.reshape(64, NK, PART), CHIPS, 1, 0)  18 us
    all_to_all x1, blocking collectives, gather(): lax.all_to_all(jnp.broadcast_to(x[None], (size, *x.shape)), axes, 0, 0, t...  17.2 us
    all_to_all x1, blocking collectives, per_device(): return lax.all_to_all(out, CHIPS, 0, 1).reshape(64, CELLS)  14 us
    ppermute x3, starting transfers between devices, per_device(): part = part + lax.ppermute(part, 'z', [(i, i ^ step) for i in range(8)])  10.5 us
    ppermute x2, starting transfers between devices, swap(): return lax.ppermute(x, 'core', [(0, 1), (1, 0)])  7.34 us
    ppermute x3, waiting for transfers between devices, per_device(): part = part + lax.ppermute(part, 'z', [(i, i ^ step) for i in range(8)])  5.96 us
  transfers between devices with their start and end apart: 5, of which 4 were waited for; matrix products, arithmetic and copies ran while one was open for 0% of the time, Pallas kernels for 1%

profile of v6, /device:TPU:1, one launch (start us, length us, event | category | flops | bytes accessed | tf_op | source)
XLA Modules:
  0.0 136.4 jit_solution(7950111361321269983)
XLA Ops:
  0.0 1.2 copy.10
  1.2 0.0 copy-start
  1.2 0.0 copy-start.1
  1.2 0.0 copy-start.2
  1.3 0.2 copy.7
  1.4 18.0 %all_to_all.40 = bf16[1,64,8,512]{3,1,0,2:T(8,128)(2,1)S(1)} all-to-all(bf16[1,64,8,512]{3,1,0,2:T(8,128)(2,1)S(1)} %copy.7), channel_id=1, replica_groups=mesh['yh'=2,'x'=4,'core'=2,'z'=8,'yl'=2] {'yh','x'}, dimensions={2} | all-to-all | bytes 1048576 | tf_op jit(solution)/shard_map/all_to_all | solution.py:348
  19.4 1.9 %collective-permute-start = (bf16[8,64,512]{2,1,0:T(8,128)(2,1)S(1)}, bf16[8,64,512]{2,1,0:T(8,128)(2,1)S(1)}, u32[]{:S(2)}, u32[]{:S(2)}) collective-permute-start(bf16[8,64,512]{2,1,0:T(8,128)(2,1)S(1)} %bitcast.29), channel_id=1, source_target_pairs={{0,16},{16,0},{1,17},{17,1},{2,18},{18,2},{3,19},{19,3},{4,20},{20... | collective-permute-start | bytes 1572872 | tf_op jit(solution)/shard_map/ppermute | solution.py:334
  21.2 0.1 pad_add_fusion.scal
  21.3 0.0 copy-done
  21.3 0.0 copy-done.1
  21.3 0.0 copy-done.2
  21.3 1.8 %obs_sums.1.ws_ref = f32[8,512]{1,0:T(8,128)S(1)} custom-call(s32[3]{0:T(128)S(1)} %pad_add_fusion.scal, s32[64,128]{1,0:T(8,128)S(1)} %bitcast.33, f32[64,128]{1,0:T(8,128)S(1)} %bitcast.34, f32[64,128]{1,0:T(8,128)S(1)} %bitcast.35), custom_call_target="tpu_custom_call" | custom-call | flops 67108864 | bytes 200000 | tf_op jit(solution)/shard_map/obs_sums/pallas_call | solution.py:69
  23.1 0.0 collective-permute-done.xb
  23.1 2.0 %gram_part.1 = (f32[16,152,128]{2,1,0:T(8,128)S(1)}, f32[8,512]{1,0:T(8,128)S(1)}) custom-call(s32[3]{0:T(128)S(1)} %pad_add_fusion.scal, f32[8,512]{1,0:T(8,128)S(1)} %obs_sums.1.ws_ref, bf16[8,64,512]{2,1,0:T(8,128)(2,1)S(1)} %bitcast.30, bf16[8,64,512]{2,1,0:T(8,128)(2,1)S(1)} %collective-permute-done.xb), custom_call_target="tpu_custom_call" | custom-call | flops 301989888 | bytes 3145728 | tf_op jit(solution)/shard_map/gram_part/pallas_call | solution.py:116
  25.2 21.3 %all_to_all.41 = f32[16,152,128]{2,1,0:T(8,128)S(1)} all-to-all(f32[16,152,128]{2,1,0:T(8,128)S(1)} %get-tuple-element.7), channel_id=1, replica_groups=mesh['yh'=2,'x'=4,'core'=2,'z'=8,'yl'=2] {'yh','x','yl'}, dimensions={0} | all-to-all | bytes 2490368 | tf_op jit(solution)/shard_map/all_to_all | solution.py:352
  46.5 0.1 reduce_sum.9
  46.6 1.7 %collective-permute-start.1 = (f32[152,128]{1,0:T(8,128)S(1)}, f32[152,128]{1,0:T(8,128)S(1)}, u32[]{:S(2)}, u32[]{:S(2)}) collective-permute-start(f32[152,128]{1,0:T(8,128)S(1)} %reduce_sum.9), channel_id=1, source_target_pairs={{0,2},{2,0},{4,6},{6,4},{8,10},{10,8},{12,14},{14,12},{1,3},{3,1},... | collective-permute-start | bytes 233480 | tf_op jit(solution)/shard_map/ppermute | solution.py:354
  48.3 1.8 %collective-permute-done.1 = f32[152,128]{1,0:T(8,128)S(1)} collective-permute-done((f32[152,128]{1,0:T(8,128)S(1)}, f32[152,128]{1,0:T(8,128)S(1)}, u32[]{:S(2)}, u32[]{:S(2)}) %collective-permute-start.1) | collective-permute-done | bytes 77856 | tf_op jit(solution)/shard_map/ppermute | solution.py:354
  50.1 3.1 %collective-permute-start.2 = (f32[152,128]{1,0:T(8,128)S(1)}, f32[152,128]{1,0:T(8,128)S(1)}, u32[]{:S(2)}, u32[]{:S(2)}) collective-permute-start(f32[152,128]{1,0:T(8,128)S(1)} %add.9), channel_id=1, source_target_pairs={{0,4},{2,6},{4,0},{6,2},{8,12},{10,14},{12,8},{14,10},{1,5},{3,7},... | collective-permute-start | bytes 233480 | tf_op jit(solution)/shard_map/ppermute | solution.py:354
  53.2 1.8 %collective-permute-done.2 = f32[152,128]{1,0:T(8,128)S(1)} collective-permute-done((f32[152,128]{1,0:T(8,128)S(1)}, f32[152,128]{1,0:T(8,128)S(1)}, u32[]{:S(2)}, u32[]{:S(2)}) %collective-permute-start.2) | collective-permute-done | bytes 77856 | tf_op jit(solution)/shard_map/ppermute | solution.py:354
  55.0 5.7 %collective-permute-start.3 = (f32[152,128]{1,0:T(8,128)S(1)}, f32[152,128]{1,0:T(8,128)S(1)}, u32[]{:S(2)}, u32[]{:S(2)}) collective-permute-start(f32[152,128]{1,0:T(8,128)S(1)} %add.10), channel_id=1, source_target_pairs={{0,14},{2,12},{4,10},{6,8},{8,6},{10,4},{12,2},{14,0},{1,15},{3,13... | collective-permute-start | bytes 233480 | tf_op jit(solution)/shard_map/ppermute | solution.py:354
  60.7 2.4 %collective-permute-done.3 = f32[152,128]{1,0:T(8,128)S(1)} collective-permute-done((f32[152,128]{1,0:T(8,128)S(1)}, f32[152,128]{1,0:T(8,128)S(1)}, u32[]{:S(2)}, u32[]{:S(2)}) %collective-permute-start.3) | collective-permute-done | bytes 77856 | tf_op jit(solution)/shard_map/ppermute | solution.py:354
  63.1 0.1 broadcast_in_dim.4
  63.2 17.2 %all_to_all.42 = f32[16,144,128]{2,1,0:T(8,128)S(1)} all-to-all(f32[16,144,128]{2,1,0:T(8,128)S(1)} %broadcast_in_dim.4), channel_id=1, replica_groups=mesh['yh'=2,'x'=4,'core'=2,'z'=8,'yl'=2] {'yh','x','yl'}, dimensions={0} | all-to-all | bytes 2359296 | tf_op jit(solution)/shard_map/all_to_all | solution.py:342
  80.4 5.5 %collective-permute-start.4 = (f32[2304,128]{1,0:T(8,128)S(1)}, f32[2304,128]{1,0:T(8,128)S(1)}, u32[]{:S(2)}, u32[]{:S(2)}) collective-permute-start(f32[2304,128]{1,0:T(8,128)S(1)} %bitcast.27), channel_id=1, source_target_pairs={{0,16},{16,0},{1,17},{17,1},{2,18},{18,2},{3,19},{19,3},{4,20},{20... | collective-permute-start | bytes 3538952 | tf_op jit(solution)/shard_map/ppermute | solution.py:334
  85.9 2.5 %collective-permute-done.4.gb = f32[2304,128]{1,0:T(8,128)S(1)} collective-permute-done((f32[2304,128]{1,0:T(8,128)S(1)}, f32[2304,128]{1,0:T(8,128)S(1)}, u32[]{:S(2)}, u32[]{:S(2)}) %collective-permute-start.4) | collective-permute-done | bytes 1179680 | tf_op jit(solution)/shard_map/ppermute | solution.py:334
  88.3 33.1 %transform.1 = bf16[8,64,512]{2,1,0:T(8,128)(2,1)S(1)} custom-call(s32[3]{0:T(128)S(1)} %pad_add_fusion.scal, f32[2304,128]{1,0:T(8,128)S(1)} %bitcast.28, f32[2304,128]{1,0:T(8,128)S(1)} %collective-permute-done.4.gb, f32[8,128]{1,0:T(8,128)S(1)} %slice.9.drive_ref, bf16[8,64,512]{2,1,0:T(8,128)(2,1)S(1)} %bitcast.31, ...), custom_call_target="tpu_custom_call" | custom-call | flops 10000000000 | bytes 4194304 | tf_op jit(solution)/shard_map/transform/pallas_call | solution.py:311
  121.5 14.0 %all_to_all.43 = bf16[8,64,1,512]{3,1,2,0:T(8,128)(2,1)S(1)} all-to-all(bf16[8,64,1,512]{3,1,2,0:T(8,128)(2,1)S(1)} %bitcast.32), channel_id=1, replica_groups=mesh['yh'=2,'x'=4,'core'=2,'z'=8,'yl'=2] {'yh','x'}, dimensions={0} | all-to-all | bytes 1048576 | tf_op jit(solution)/shard_map/all_to_all | solution.py:358
  135.5 0.8 copy.11
  (5 shorter events, 0.0 us)
Async XLA Ops:
  1.2 20.1 %copy-start = (s32[8192]{0:T(1024)S(1)}, s32[8192]{0:T(1024)}, u32[]{:S(2)}) copy-start(s32[8192]{0:T(1024)} %param.5) | copy-start | bytes 98308
  1.2 20.1 %copy-start.1 = (f32[8192]{0:T(1024)S(1)}, f32[8192]{0:T(1024)}, u32[]{:S(2)}) copy-start(f32[8192]{0:T(1024)} %param.6) | copy-start | bytes 98308
  1.2 20.1 %copy-start.2 = (f32[8192]{0:T(1024)S(1)}, f32[8192]{0:T(1024)}, u32[]{:S(2)}) copy-start(f32[8192]{0:T(1024)} %param.7) | copy-start | bytes 98308
  19.4 3.8 %collective-permute-start = (bf16[8,64,512]{2,1,0:T(8,128)(2,1)S(1)}, bf16[8,64,512]{2,1,0:T(8,128)(2,1)S(1)}, u32[]{:S(2)}, u32[]{:S(2)}) collective-permute-start(bf16[8,64,512]{2,1,0:T(8,128)(2,1)S(1)} %bitcast.29), channel_id=1, source_target_pairs={{0,16},{16,0},{1,17},{17,1},{2,18},{18,2},{3,19},{19,3},{4,20},{20... | collective-permute-start | bytes 1572872 | tf_op jit(solution)/shard_map/ppermute | solution.py:334
  46.6 3.5 %collective-permute-start.1 = (f32[152,128]{1,0:T(8,128)S(1)}, f32[152,128]{1,0:T(8,128)S(1)}, u32[]{:S(2)}, u32[]{:S(2)}) collective-permute-start(f32[152,128]{1,0:T(8,128)S(1)} %reduce_sum.9), channel_id=1, source_target_pairs={{0,2},{2,0},{4,6},{6,4},{8,10},{10,8},{12,14},{14,12},{1,3},{3,1},... | collective-permute-start | bytes 233480 | tf_op jit(solution)/shard_map/ppermute | solution.py:354
  50.1 4.9 %collective-permute-start.2 = (f32[152,128]{1,0:T(8,128)S(1)}, f32[152,128]{1,0:T(8,128)S(1)}, u32[]{:S(2)}, u32[]{:S(2)}) collective-permute-start(f32[152,128]{1,0:T(8,128)S(1)} %add.9), channel_id=1, source_target_pairs={{0,4},{2,6},{4,0},{6,2},{8,12},{10,14},{12,8},{14,10},{1,5},{3,7},... | collective-permute-start | bytes 233480 | tf_op jit(solution)/shard_map/ppermute | solution.py:354
  55.0 8.1 %collective-permute-start.3 = (f32[152,128]{1,0:T(8,128)S(1)}, f32[152,128]{1,0:T(8,128)S(1)}, u32[]{:S(2)}, u32[]{:S(2)}) collective-permute-start(f32[152,128]{1,0:T(8,128)S(1)} %add.10), channel_id=1, source_target_pairs={{0,14},{2,12},{4,10},{6,8},{8,6},{10,4},{12,2},{14,0},{1,15},{3,13... | collective-permute-start | bytes 233480 | tf_op jit(solution)/shard_map/ppermute | solution.py:354
  80.4 7.9 %collective-permute-start.4 = (f32[2304,128]{1,0:T(8,128)S(1)}, f32[2304,128]{1,0:T(8,128)S(1)}, u32[]{:S(2)}, u32[]{:S(2)}) collective-permute-start(f32[2304,128]{1,0:T(8,128)S(1)} %bitcast.27), channel_id=1, source_target_pairs={{0,16},{16,0},{1,17},{17,1},{2,18},{18,2},{3,19},{19,3},{4,20},{20... | collective-permute-start | bytes 3538952 | tf_op jit(solution)/shard_map/ppermute | solution.py:334

commit v7 on v6

--- a/solution.py
+++ b/solution.py
@@ -198,26 +198,34 @@
         for i, x in enumerate([h, m, h, l, h, m]):
             rhs[side, blk(i), blk(j, n)] = x
 
+    def put_inverse(side, j, n, r):
+        h, m, _ = split3(r)
+        for i, x in enumerate([h, m, h]):
+            rhs[side, blk(i), blk(j, n)] = x
+
     def own(k):
         v = vb[k % 2]
         z[blk(k), blk(k)] = v
-        put(k % 2, k, 1, v)
+        put_inverse(k % 2, k, 1, v)
 
     def row(k, j, n):
         side = k % 2
         h, m, l = split3(z[blk(k), blk(j, n)])
+        if j < k:
+            r = jnp.dot(ab[side, :, blk(0, 3)], jnp.concatenate([h, m, h], axis=0), preferred_element_type=F32)
+            put_inverse(side, j, n, r)
+            z[blk(k), blk(j, n)] = r
+            return
         r = jnp.dot(ab[side], jnp.concatenate([h, m, h, l, h, m], axis=0), preferred_element_type=F32)
         put(side, j, n, r)
-        if j < k:
-            z[blk(k), blk(j, n)] = r
-            return
         for q in range(n):
             x = split3(r[:, blk(q)].T)
             for i, t in enumerate([0, 0, 1, 0, 2, 1]):
                 lhs[side, blk(j + q), blk(i)] = x[t]
 
-    def reduce(side, i, m, j, n):
-        prod = jnp.dot(lhs[side, blk(i, m), :], rhs[side, :, blk(j, n)], preferred_element_type=F32)
+    def reduce(side, i, m, j, n, terms=6):
+        cut = blk(0, terms)
+        prod = jnp.dot(lhs[side, blk(i, m), cut], rhs[side, cut, blk(j, n)], preferred_element_type=F32)
         z[blk(i, m), blk(j, n)] = z[blk(i, m), blk(j, n)] - prod
 
     pending = []
@@ -244,12 +252,12 @@
             later(row, k, j, min(2, NK - j))
         if k + 1 < NK:
             for j in range(0, k + 1, 2):
-                later(reduce, side, k + 1, 1, j, min(2, k + 1 - j))
+                later(reduce, side, k + 1, 1, j, min(2, k + 1 - j), 3)
             for j in range(k + 2, NK, 2):
                 later(reduce, side, k + 1, 1, j, min(2, NK - j))
         for j in range(0, k + 1, 2):
             for i in range(k + 2, NK, 3):
-                later(reduce, side, i, min(3, NK - i), j, min(2, k + 1 - j))
+                later(reduce, side, i, min(3, NK - i), j, min(2, k + 1 - j), 3)
         for j in range(k + 2, NK, 2):
             n = min(2, NK - j)
             for i in range(k + 2, j + 1, 3):

time: 137 us -> 136 us (level)
  no operation moved by 1% of the time
where the time goes in v7:
time: 136 us
  blocking collectives  70.5 us (52%)
  Pallas kernels  36.8 us (27%)
  starting transfers between devices  17.8 us (13%)
  waiting for transfers between devices  8.43 us (6%)
  local copies, waits for them, and re-layouts  2.31 us (2%)
    pallas_call x1, Pallas kernels, transform(): pl.pallas_call(transform_kernel, out_shape=jax.ShapeDtypeStruct((NK, 64,...  32.9 us
    all_to_all x1, blocking collectives, per_device(): part = jnp.sum(lax.all_to_all(part, PLANE, 0, 0, tiled=True), axis=0)  21.3 us
    all_to_all x1, blocking collectives, per_device(): xa = lax.all_to_all(background_samples.reshape(64, NK, PART), CHIPS, 1, 0)  18 us
    all_to_all x1, blocking collectives, gather(): lax.all_to_all(jnp.broadcast_to(x[None], (size, *x.shape)), axes, 0, 0, t...  17.2 us
    all_to_all x1, blocking collectives, per_device(): return lax.all_to_all(out, CHIPS, 0, 1).reshape(64, CELLS)  14 us
    ppermute x3, starting transfers between devices, per_device(): part = part + lax.ppermute(part, 'z', [(i, i ^ step) for i in range(8)])  10.5 us
    ppermute x2, starting transfers between devices, swap(): return lax.ppermute(x, 'core', [(0, 1), (1, 0)])  7.34 us
    ppermute x3, waiting for transfers between devices, per_device(): part = part + lax.ppermute(part, 'z', [(i, i ^ step) for i in range(8)])  5.96 us
  transfers between devices with their start and end apart: 5, of which 4 were waited for; matrix products, arithmetic and copies ran while one was open for 0% of the time, Pallas kernels for 1%

profile of v7, /device:TPU:1, one launch (start us, length us, event | category | flops | bytes accessed | tf_op | source)
XLA Modules:
  0.0 136.1 jit_solution(3971398138829941332)
XLA Ops:
  0.0 1.2 copy.10
  1.2 0.0 copy-start
  1.2 0.0 copy-start.1
  1.2 0.0 copy-start.2
  1.3 0.2 copy.7
  1.4 18.0 %all_to_all.40 = bf16[1,64,8,512]{3,1,0,2:T(8,128)(2,1)S(1)} all-to-all(bf16[1,64,8,512]{3,1,0,2:T(8,128)(2,1)S(1)} %copy.7), channel_id=1, replica_groups=mesh['yh'=2,'x'=4,'core'=2,'z'=8,'yl'=2] {'yh','x'}, dimensions={2} | all-to-all | bytes 1048576 | tf_op jit(solution)/shard_map/all_to_all | solution.py:356
  19.4 1.9 %collective-permute-start = (bf16[8,64,512]{2,1,0:T(8,128)(2,1)S(1)}, bf16[8,64,512]{2,1,0:T(8,128)(2,1)S(1)}, u32[]{:S(2)}, u32[]{:S(2)}) collective-permute-start(bf16[8,64,512]{2,1,0:T(8,128)(2,1)S(1)} %bitcast.29), channel_id=1, source_target_pairs={{0,16},{16,0},{1,17},{17,1},{2,18},{18,2},{3,19},{19,3},{4,20},{20... | collective-permute-start | bytes 1572872 | tf_op jit(solution)/shard_map/ppermute | solution.py:342
  21.2 0.1 pad_add_fusion.scal
  21.3 0.0 copy-done
  21.3 0.0 copy-done.1
  21.3 0.0 copy-done.2
  21.3 1.8 %obs_sums.1.ws_ref = f32[8,512]{1,0:T(8,128)S(1)} custom-call(s32[3]{0:T(128)S(1)} %pad_add_fusion.scal, s32[64,128]{1,0:T(8,128)S(1)} %bitcast.33, f32[64,128]{1,0:T(8,128)S(1)} %bitcast.34, f32[64,128]{1,0:T(8,128)S(1)} %bitcast.35), custom_call_target="tpu_custom_call" | custom-call | flops 67108864 | bytes 200000 | tf_op jit(solution)/shard_map/obs_sums/pallas_call | solution.py:69
  23.1 0.0 collective-permute-done.xb
  23.1 2.0 %gram_part.1 = (f32[16,152,128]{2,1,0:T(8,128)S(1)}, f32[8,512]{1,0:T(8,128)S(1)}) custom-call(s32[3]{0:T(128)S(1)} %pad_add_fusion.scal, f32[8,512]{1,0:T(8,128)S(1)} %obs_sums.1.ws_ref, bf16[8,64,512]{2,1,0:T(8,128)(2,1)S(1)} %bitcast.30, bf16[8,64,512]{2,1,0:T(8,128)(2,1)S(1)} %collective-permute-done.xb), custom_call_target="tpu_custom_call" | custom-call | flops 301989888 | bytes 3145728 | tf_op jit(solution)/shard_map/gram_part/pallas_call | solution.py:116
  25.2 21.3 %all_to_all.41 = f32[16,152,128]{2,1,0:T(8,128)S(1)} all-to-all(f32[16,152,128]{2,1,0:T(8,128)S(1)} %get-tuple-element.7), channel_id=1, replica_groups=mesh['yh'=2,'x'=4,'core'=2,'z'=8,'yl'=2] {'yh','x','yl'}, dimensions={0} | all-to-all | bytes 2490368 | tf_op jit(solution)/shard_map/all_to_all | solution.py:360
  46.5 0.1 reduce_sum.9
  46.6 1.7 %collective-permute-start.1 = (f32[152,128]{1,0:T(8,128)S(1)}, f32[152,128]{1,0:T(8,128)S(1)}, u32[]{:S(2)}, u32[]{:S(2)}) collective-permute-start(f32[152,128]{1,0:T(8,128)S(1)} %reduce_sum.9), channel_id=1, source_target_pairs={{0,2},{2,0},{4,6},{6,4},{8,10},{10,8},{12,14},{14,12},{1,3},{3,1},... | collective-permute-start | bytes 233480 | tf_op jit(solution)/shard_map/ppermute | solution.py:362
  48.3 1.8 %collective-permute-done.1 = f32[152,128]{1,0:T(8,128)S(1)} collective-permute-done((f32[152,128]{1,0:T(8,128)S(1)}, f32[152,128]{1,0:T(8,128)S(1)}, u32[]{:S(2)}, u32[]{:S(2)}) %collective-permute-start.1) | collective-permute-done | bytes 77856 | tf_op jit(solution)/shard_map/ppermute | solution.py:362
  50.1 3.1 %collective-permute-start.2 = (f32[152,128]{1,0:T(8,128)S(1)}, f32[152,128]{1,0:T(8,128)S(1)}, u32[]{:S(2)}, u32[]{:S(2)}) collective-permute-start(f32[152,128]{1,0:T(8,128)S(1)} %add.9), channel_id=1, source_target_pairs={{0,4},{2,6},{4,0},{6,2},{8,12},{10,14},{12,8},{14,10},{1,5},{3,7},... | collective-permute-start | bytes 233480 | tf_op jit(solution)/shard_map/ppermute | solution.py:362
  53.2 1.8 %collective-permute-done.2 = f32[152,128]{1,0:T(8,128)S(1)} collective-permute-done((f32[152,128]{1,0:T(8,128)S(1)}, f32[152,128]{1,0:T(8,128)S(1)}, u32[]{:S(2)}, u32[]{:S(2)}) %collective-permute-start.2) | collective-permute-done | bytes 77856 | tf_op jit(solution)/shard_map/ppermute | solution.py:362
  55.0 5.7 %collective-permute-start.3 = (f32[152,128]{1,0:T(8,128)S(1)}, f32[152,128]{1,0:T(8,128)S(1)}, u32[]{:S(2)}, u32[]{:S(2)}) collective-permute-start(f32[152,128]{1,0:T(8,128)S(1)} %add.10), channel_id=1, source_target_pairs={{0,14},{2,12},{4,10},{6,8},{8,6},{10,4},{12,2},{14,0},{1,15},{3,13... | collective-permute-start | bytes 233480 | tf_op jit(solution)/shard_map/ppermute | solution.py:362
  60.7 2.4 %collective-permute-done.3 = f32[152,128]{1,0:T(8,128)S(1)} collective-permute-done((f32[152,128]{1,0:T(8,128)S(1)}, f32[152,128]{1,0:T(8,128)S(1)}, u32[]{:S(2)}, u32[]{:S(2)}) %collective-permute-start.3) | collective-permute-done | bytes 77856 | tf_op jit(solution)/shard_map/ppermute | solution.py:362
  63.1 0.1 broadcast_in_dim.4
  63.2 17.2 %all_to_all.42 = f32[16,144,128]{2,1,0:T(8,128)S(1)} all-to-all(f32[16,144,128]{2,1,0:T(8,128)S(1)} %broadcast_in_dim.4), channel_id=1, replica_groups=mesh['yh'=2,'x'=4,'core'=2,'z'=8,'yl'=2] {'yh','x','yl'}, dimensions={0} | all-to-all | bytes 2359296 | tf_op jit(solution)/shard_map/all_to_all | solution.py:350
  80.4 5.5 %collective-permute-start.4 = (f32[2304,128]{1,0:T(8,128)S(1)}, f32[2304,128]{1,0:T(8,128)S(1)}, u32[]{:S(2)}, u32[]{:S(2)}) collective-permute-start(f32[2304,128]{1,0:T(8,128)S(1)} %bitcast.27), channel_id=1, source_target_pairs={{0,16},{16,0},{1,17},{17,1},{2,18},{18,2},{3,19},{19,3},{4,20},{20... | collective-permute-start | bytes 3538952 | tf_op jit(solution)/shard_map/ppermute | solution.py:342
  85.9 2.5 %collective-permute-done.4.gb = f32[2304,128]{1,0:T(8,128)S(1)} collective-permute-done((f32[2304,128]{1,0:T(8,128)S(1)}, f32[2304,128]{1,0:T(8,128)S(1)}, u32[]{:S(2)}, u32[]{:S(2)}) %collective-permute-start.4) | collective-permute-done | bytes 1179680 | tf_op jit(solution)/shard_map/ppermute | solution.py:342
  88.3 32.9 %transform.1 = bf16[8,64,512]{2,1,0:T(8,128)(2,1)S(1)} custom-call(s32[3]{0:T(128)S(1)} %pad_add_fusion.scal, f32[2304,128]{1,0:T(8,128)S(1)} %bitcast.28, f32[2304,128]{1,0:T(8,128)S(1)} %collective-permute-done.4.gb, f32[8,128]{1,0:T(8,128)S(1)} %slice.9.drive_ref, bf16[8,64,512]{2,1,0:T(8,128)(2,1)S(1)} %bitcast.31, ...), custom_call_target="tpu_custom_call" | custom-call | flops 10000000000 | bytes 4194304 | tf_op jit(solution)/shard_map/transform/pallas_call | solution.py:319
  121.3 14.0 %all_to_all.43 = bf16[8,64,1,512]{3,1,2,0:T(8,128)(2,1)S(1)} all-to-all(bf16[8,64,1,512]{3,1,2,0:T(8,128)(2,1)S(1)} %bitcast.32), channel_id=1, replica_groups=mesh['yh'=2,'x'=4,'core'=2,'z'=8,'yl'=2] {'yh','x'}, dimensions={0} | all-to-all | bytes 1048576 | tf_op jit(solution)/shard_map/all_to_all | solution.py:366
  135.3 0.8 copy.11
  (5 shorter events, 0.0 us)
Async XLA Ops:
  1.2 20.1 %copy-start = (s32[8192]{0:T(1024)S(1)}, s32[8192]{0:T(1024)}, u32[]{:S(2)}) copy-start(s32[8192]{0:T(1024)} %param.5) | copy-start | bytes 98308
  1.2 20.1 %copy-start.1 = (f32[8192]{0:T(1024)S(1)}, f32[8192]{0:T(1024)}, u32[]{:S(2)}) copy-start(f32[8192]{0:T(1024)} %param.6) | copy-start | bytes 98308
  1.2 20.1 %copy-start.2 = (f32[8192]{0:T(1024)S(1)}, f32[8192]{0:T(1024)}, u32[]{:S(2)}) copy-start(f32[8192]{0:T(1024)} %param.7) | copy-start | bytes 98308
  19.4 3.8 %collective-permute-start = (bf16[8,64,512]{2,1,0:T(8,128)(2,1)S(1)}, bf16[8,64,512]{2,1,0:T(8,128)(2,1)S(1)}, u32[]{:S(2)}, u32[]{:S(2)}) collective-permute-start(bf16[8,64,512]{2,1,0:T(8,128)(2,1)S(1)} %bitcast.29), channel_id=1, source_target_pairs={{0,16},{16,0},{1,17},{17,1},{2,18},{18,2},{3,19},{19,3},{4,20},{20... | collective-permute-start | bytes 1572872 | tf_op jit(solution)/shard_map/ppermute | solution.py:342
  46.6 3.5 %collective-permute-start.1 = (f32[152,128]{1,0:T(8,128)S(1)}, f32[152,128]{1,0:T(8,128)S(1)}, u32[]{:S(2)}, u32[]{:S(2)}) collective-permute-start(f32[152,128]{1,0:T(8,128)S(1)} %reduce_sum.9), channel_id=1, source_target_pairs={{0,2},{2,0},{4,6},{6,4},{8,10},{10,8},{12,14},{14,12},{1,3},{3,1},... | collective-permute-start | bytes 233480 | tf_op jit(solution)/shard_map/ppermute | solution.py:362
  50.1 4.9 %collective-permute-start.2 = (f32[152,128]{1,0:T(8,128)S(1)}, f32[152,128]{1,0:T(8,128)S(1)}, u32[]{:S(2)}, u32[]{:S(2)}) collective-permute-start(f32[152,128]{1,0:T(8,128)S(1)} %add.9), channel_id=1, source_target_pairs={{0,4},{2,6},{4,0},{6,2},{8,12},{10,14},{12,8},{14,10},{1,5},{3,7},... | collective-permute-start | bytes 233480 | tf_op jit(solution)/shard_map/ppermute | solution.py:362
  55.0 8.1 %collective-permute-start.3 = (f32[152,128]{1,0:T(8,128)S(1)}, f32[152,128]{1,0:T(8,128)S(1)}, u32[]{:S(2)}, u32[]{:S(2)}) collective-permute-start(f32[152,128]{1,0:T(8,128)S(1)} %add.10), channel_id=1, source_target_pairs={{0,14},{2,12},{4,10},{6,8},{8,6},{10,4},{12,2},{14,0},{1,15},{3,13... | collective-permute-start | bytes 233480 | tf_op jit(solution)/shard_map/ppermute | solution.py:362
  80.4 7.9 %collective-permute-start.4 = (f32[2304,128]{1,0:T(8,128)S(1)}, f32[2304,128]{1,0:T(8,128)S(1)}, u32[]{:S(2)}, u32[]{:S(2)}) collective-permute-start(f32[2304,128]{1,0:T(8,128)S(1)} %bitcast.27), channel_id=1, source_target_pairs={{0,16},{16,0},{1,17},{17,1},{2,18},{18,2},{3,19},{19,3},{4,20},{20... | collective-permute-start | bytes 3538952 | tf_op jit(solution)/shard_map/ppermute | solution.py:342
